TPU v7x, 32 devices: a whole 2x2x4 slice. The times are simulated.
32 devices in a mesh: dp: 8 (over y, x, core), section: 4 (over z).
Axes of the slice: x: 2, y: 2, z: 4, core: 2. Of those that a mesh axis runs over, the one named last changes fastest.
Arguments:
- tokens: bfloat16 [16, 1024, 768], P('dp'), may hold values from -6 to 6
- span_start: int32 [16], P('dp'), may hold values from 0 to 511
- span_length: int32 [16], P('dp'), may hold values from 1 to 512
- time_step: int32 [16], P('dp'), may hold values from 0 to 511
- time_table: float32 [512, 128], replicated, may hold values from -6 to 6
- mask_embed: bfloat16 [768], replicated, may hold values from -6 to 6
- mod_weight: float32 [4, 128, 2304], P('section'), may hold values from -0.5 to 0.5
- mod_bias: float32 [4, 2304], P('section'), may hold values from -3 to 3
- norm_gain: float32 [4, 768], P('section'), may hold values from 0.5 to 1.5
- in_weight: bfloat16 [4, 768, 3072], P('section')
- in_bias: float32 [4, 3072], P('section'), may hold values from -2 to 2
- out_weight: bfloat16 [4, 3072, 768], P('section'), may hold values from -0.109375 to 0.109375
- out_bias: float32 [4, 768], P('section'), may hold values from -2 to 2
- cotangent: bfloat16 [16, 1024, 768], P('dp'), may hold values from -6 to 6
Outputs:
- hidden_states: bfloat16 [4, 16, 1024, 768], P('section', 'dp')
- stream_grads: bfloat16 [4, 16, 1024, 768], P('section', 'dp')
- time_table_grad: float32 [512, 128], replicated
- mask_embed_grad: float32 [768], replicated
- mod_weight_grad: float32 [4, 128, 2304], P('section')
- mod_bias_grad: float32 [4, 2304], P('section')
- norm_gain_grad: float32 [4, 768], P('section')
- in_weight_grad: float32 [4, 768, 3072], P('section')
- in_bias_grad: float32 [4, 3072], P('section')
- out_weight_grad: float32 [4, 3072, 768], P('section')
- out_bias_grad: float32 [4, 768], P('section')
All inputs are finite; a program needn't handle non-finite values.
Results may differ from a plain program's by a relative error of at most 0.015.
The roundings to bfloat16 on the way count: a program that leaves them out, or rounds other values in their place, can miss the bound.
Values may be sent and summed in bfloat16 or wider, within the bound.
A program may use at most 256 MiB of HBM per device.

v0:
```python
from functools import partial
import math

import jax
import jax.numpy as jnp
from jax import lax
from jax.sharding import PartitionSpec as P

HEAD = 64


EPS = 1e-06
HIGH = lax.Precision.HIGHEST
F32 = jnp.float32
BF16 = jnp.bfloat16


def shifted(value, axis, steps):
    count = lax.axis_size(axis)
    first, last = (max(0, -steps), min(count, count - steps))
    return lax.ppermute(value, axis, [(source, source + steps) for source in range(first, last)])


def rope_tables(length, head_size):
    half_head = head_size // 2
    position = lax.broadcasted_iota(F32, (length, half_head), 0)
    column = lax.broadcasted_iota(F32, (length, half_head), 1)
    angles = position * jnp.exp(column * (-2.0 * math.log(10000.0) / head_size))
    return (jnp.cos(angles)[:, None, :], jnp.sin(angles)[:, None, :])


def rotate(values, cosine_table, sine_table):
    half_head = values.shape[-1] // 2
    front_half = values[..., :half_head]
    back_half = values[..., half_head:]
    return jnp.concatenate(
        [
            front_half * cosine_table - back_half * sine_table,
            back_half * cosine_table + front_half * sine_table,
        ],
        -1,
    )


def rotate_back(gradient, cosine_table, sine_table):
    half_head = gradient.shape[-1] // 2
    front_half = gradient[..., :half_head]
    back_half = gradient[..., half_head:]
    return jnp.concatenate(
        [
            front_half * cosine_table + back_half * sine_table,
            back_half * cosine_table - front_half * sine_table,
        ],
        -1,
    )


def modulate(current, modulation_row, gain_row):
    features = current.shape[1]
    shifting = modulation_row[:features]
    scaling = modulation_row[features : 2 * features]
    gating = modulation_row[2 * features :]
    average = jnp.mean(current, -1, keepdims=True)
    centered = current - average
    inverse_std = lax.rsqrt(jnp.mean(centered * centered, -1, keepdims=True) + EPS)
    standard = centered * inverse_std
    normalized = standard * gain_row
    modulated_rows = (normalized * (1.0 + scaling) + shifting).astype(BF16)
    return (standard, inverse_std, normalized, modulated_rows, scaling, gating)


def modulate_back(grad_rows, standard, inverse_std, normalized, scaling, gain_row):
    grad_normed = grad_rows * (1.0 + scaling)
    grad_shift = jnp.sum(grad_rows, 0)
    grad_scale = jnp.sum(grad_rows * normalized, 0)
    grad_gain = jnp.sum(grad_normed * standard, 0)
    grad_hat = grad_normed * gain_row
    grad_current = inverse_std * (
        grad_hat
        - jnp.mean(grad_hat, -1, keepdims=True)
        - standard * jnp.mean(grad_hat * standard, -1, keepdims=True)
    )
    return (grad_current, grad_shift, grad_scale, grad_gain)


def project_heads(modulated_rows, first_matrix, first_bias):
    length, features = modulated_rows.shape
    head_count = features // HEAD
    projected = (
        jnp.dot(modulated_rows, first_matrix[:, : 3 * features], preferred_element_type=F32)
        + first_bias[: 3 * features]
    )
    cosine_table, sine_table = rope_tables(length, HEAD)
    queries = rotate(
        projected[:, :features].reshape(length, head_count, HEAD), cosine_table, sine_table
    ).astype(BF16)
    key_rows = rotate(
        projected[:, features : 2 * features].reshape(length, head_count, HEAD),
        cosine_table,
        sine_table,
    ).astype(BF16)
    value_rows = projected[:, 2 * features :].reshape(length, head_count, HEAD).astype(BF16)
    return (queries, key_rows, value_rows, cosine_table, sine_table)


def softmax_rows(query_block, key_rows):
    scores = jnp.einsum(
        "qhd,khd->hqk", query_block, key_rows, preferred_element_type=F32
    ) * HEAD ** (-0.5)
    row_max = jnp.max(scores, -1, keepdims=True)
    exponents = jnp.exp(scores - row_max)
    return exponents / jnp.sum(exponents, -1, keepdims=True)


def attention_mix(queries, key_rows, value_rows):
    length = queries.shape[0]
    row_block = min(512, length)
    pieces = []
    for offset in range(0, length, row_block):
        weights_low = softmax_rows(queries[offset : offset + row_block], key_rows).astype(BF16)
        pieces.append(
            jnp.einsum("hqk,khd->qhd", weights_low, value_rows, preferred_element_type=F32)
        )
    return jnp.concatenate(pieces, 0)


def empty_grads(section_params):
    return tuple((jnp.zeros(member.shape, F32) for member in section_params))


def attention_forward(current, modulation_row, section_params):
    mod_matrix, mod_vector, gain_row, first_matrix, first_bias, second_matrix, second_bias = (
        section_params
    )
    length, features = current.shape
    standard, inverse_std, normalized, modulated_rows, scaling, gating = modulate(
        current, modulation_row, gain_row
    )
    queries, key_rows, value_rows, cosine_table, sine_table = project_heads(
        modulated_rows, first_matrix, first_bias
    )
    mixed = attention_mix(queries, key_rows, value_rows).reshape(length, features).astype(BF16)
    branch = (
        jnp.dot(mixed, first_matrix[:, 3 * features :], preferred_element_type=F32)
        + first_bias[3 * features :]
    )
    return current + gating * branch


def attention_backward(current, upstream, modulation_row, condition_row, section_params):
    mod_matrix, mod_vector, gain_row, first_matrix, first_bias, second_matrix, second_bias = (
        section_params
    )
    length, features = current.shape
    head_count = features // HEAD
    scale_factor = HEAD ** (-0.5)
    standard, inverse_std, normalized, modulated_rows, scaling, gating = modulate(
        current, modulation_row, gain_row
    )
    queries, key_rows, value_rows, cosine_table, sine_table = project_heads(
        modulated_rows, first_matrix, first_bias
    )
    mixed = attention_mix(queries, key_rows, value_rows).reshape(length, features).astype(BF16)
    output_matrix = first_matrix[:, 3 * features :]
    branch = jnp.dot(mixed, output_matrix, preferred_element_type=F32) + first_bias[3 * features :]
    grad_gate = jnp.sum(upstream * branch, 0)
    grad_branch = (gating * upstream).astype(BF16)
    grad_output_matrix = jnp.einsum("tw,tv->wv", mixed, grad_branch, preferred_element_type=F32)
    grad_output_bias = jnp.sum(grad_branch.astype(F32), 0)
    grad_mixed = (
        jnp.einsum("tv,wv->tw", grad_branch, output_matrix, preferred_element_type=F32)
        .astype(BF16)
        .reshape(length, head_count, HEAD)
    )
    row_block = min(512, length)
    grad_key_sum = jnp.zeros((length, head_count, HEAD), F32)
    grad_value_sum = jnp.zeros((length, head_count, HEAD), F32)
    query_pieces = []
    for offset in range(0, length, row_block):
        query_block = queries[offset : offset + row_block]
        grad_block = grad_mixed[offset : offset + row_block]
        weights_block = softmax_rows(query_block, key_rows)
        grad_weights = jnp.einsum(
            "qhd,khd->hqk", grad_block, value_rows, preferred_element_type=F32
        )
        row_dot = jnp.sum(grad_weights * weights_block, -1, keepdims=True)
        grad_scores = (weights_block * (grad_weights - row_dot)).astype(BF16)
        query_pieces.append(
            jnp.einsum("hqk,khd->qhd", grad_scores, key_rows, preferred_element_type=F32)
            * scale_factor
        )
        grad_key_sum = grad_key_sum + jnp.einsum(
            "hqk,qhd->khd", grad_scores, query_block, preferred_element_type=F32
        )
        grad_value_sum = grad_value_sum + jnp.einsum(
            "hqk,qhd->khd", weights_block.astype(BF16), grad_block, preferred_element_type=F32
        )
    grad_queries = rotate_back(jnp.concatenate(query_pieces, 0), cosine_table, sine_table)
    grad_keys = rotate_back(grad_key_sum * scale_factor, cosine_table, sine_table)
    grad_projected = jnp.concatenate(
        [
            grad_queries.reshape(length, features),
            grad_keys.reshape(length, features),
            grad_value_sum.reshape(length, features),
        ],
        1,
    ).astype(BF16)
    grad_input_matrix = jnp.einsum(
        "tw,tv->wv", modulated_rows, grad_projected, preferred_element_type=F32
    )
    grad_input_bias = jnp.sum(grad_projected.astype(F32), 0)
    grad_rows = jnp.einsum(
        "tv,wv->tw", grad_projected, first_matrix[:, : 3 * features], preferred_element_type=F32
    )
    grad_current, grad_shift, grad_scale, grad_gain = modulate_back(
        grad_rows, standard, inverse_std, normalized, scaling, gain_row
    )
    grad_modulation = jnp.concatenate([grad_shift, grad_scale, grad_gate])
    gradients = (
        condition_row[:, None] * grad_modulation[None, :],
        grad_modulation,
        grad_gain,
        jnp.concatenate([grad_input_matrix, grad_output_matrix], 1),
        jnp.concatenate([grad_input_bias, grad_output_bias]),
        jnp.zeros(second_matrix.shape, F32),
        jnp.zeros(second_bias.shape, F32),
    )
    return (upstream + grad_current, grad_modulation, gradients)


def mlp_forward(current, modulation_row, section_params):
    mod_matrix, mod_vector, gain_row, first_matrix, first_bias, second_matrix, second_bias = (
        section_params
    )
    standard, inverse_std, normalized, modulated_rows, scaling, gating = modulate(
        current, modulation_row, gain_row
    )
    hidden = jnp.dot(modulated_rows, first_matrix, preferred_element_type=F32) + first_bias
    activated = jax.nn.gelu(hidden, approximate=True).astype(BF16)
    branch = jnp.dot(activated, second_matrix, preferred_element_type=F32) + second_bias
    return current + gating * branch


def mlp_backward(current, upstream, modulation_row, condition_row, section_params):
    mod_matrix, mod_vector, gain_row, first_matrix, first_bias, second_matrix, second_bias = (
        section_params
    )
    standard, inverse_std, normalized, modulated_rows, scaling, gating = modulate(
        current, modulation_row, gain_row
    )
    hidden = jnp.dot(modulated_rows, first_matrix, preferred_element_type=F32) + first_bias
    activated_full, gelu_pull = jax.vjp(partial(jax.nn.gelu, approximate=True), hidden)
    activated = activated_full.astype(BF16)
    branch = jnp.dot(activated, second_matrix, preferred_element_type=F32) + second_bias
    grad_gate = jnp.sum(upstream * branch, 0)
    grad_branch = (gating * upstream).astype(BF16)
    grad_second = jnp.einsum("tf,tv->fv", activated, grad_branch, preferred_element_type=F32)
    grad_second_bias = jnp.sum(grad_branch.astype(F32), 0)
    grad_activated = jnp.einsum("tv,fv->tf", grad_branch, second_matrix, preferred_element_type=F32)
    grad_hidden = gelu_pull(grad_activated)[0].astype(BF16)
    grad_first = jnp.einsum("tw,tf->wf", modulated_rows, grad_hidden, preferred_element_type=F32)
    grad_first_bias = jnp.sum(grad_hidden.astype(F32), 0)
    grad_rows = jnp.einsum("tf,wf->tw", grad_hidden, first_matrix, preferred_element_type=F32)
    grad_current, grad_shift, grad_scale, grad_gain = modulate_back(
        grad_rows, standard, inverse_std, normalized, scaling, gain_row
    )
    grad_modulation = jnp.concatenate([grad_shift, grad_scale, grad_gate])
    gradients = (
        condition_row[:, None] * grad_modulation[None, :],
        grad_modulation,
        grad_gain,
        grad_first,
        grad_first_bias,
        grad_second,
        grad_second_bias,
    )
    return (upstream + grad_current, grad_modulation, gradients)


def put_slot(buffer, slot_index, active, new_value):
    previous = lax.dynamic_index_in_dim(buffer, slot_index, 0, keepdims=False)
    return lax.dynamic_update_index_in_dim(
        buffer, jnp.where(active, new_value, previous), slot_index, 0
    )


def pick_row(array, slot_index):
    return lax.dynamic_index_in_dim(array, slot_index, 0, keepdims=False)


def shards(
    tokens,
    span_start,
    span_length,
    time_step,
    time_table,
    mask_embed,
    mod_weight,
    mod_bias,
    norm_gain,
    in_weight,
    in_bias,
    out_weight,
    out_bias,
    cotangent,
):
    section_index = lax.axis_index("section")
    sections = lax.axis_size("section")
    micro_count, length, features = tokens.shape
    tick_count = micro_count + sections - 1
    section_params = (
        mod_weight[0],
        mod_bias[0],
        norm_gain[0],
        in_weight[0],
        in_bias[0],
        out_weight[0],
        out_bias[0],
    )
    is_attention = section_index % 2 == 0
    step_onehot = (
        time_step[:, None] == lax.broadcasted_iota(jnp.int32, (micro_count, time_table.shape[0]), 1)
    ).astype(F32)
    embedded = jnp.dot(step_onehot, time_table, precision=HIGH)
    conditions = jax.nn.silu(embedded)
    modulations = jnp.dot(conditions, mod_weight[0], precision=HIGH) + mod_bias[0]
    position = lax.broadcasted_iota(jnp.int32, (micro_count, length), 1)
    in_span = (position >= span_start[:, None]) & (position < (span_start + span_length)[:, None])
    first_inputs = jnp.where(in_span[:, :, None], mask_embed[None, None, :], tokens)

    def run_forward(current, modulation_row):
        return lax.cond(
            is_attention, attention_forward, mlp_forward, current, modulation_row, section_params
        )

    def run_backward(current, upstream, modulation_row, condition_row):
        return lax.cond(
            is_attention,
            attention_backward,
            mlp_backward,
            current,
            upstream,
            modulation_row,
            condition_row,
            section_params,
        )

    def forward_tick(tick_number, carried):
        arrived, stored, states = carried
        slot_number = tick_number - section_index
        active = (slot_number >= 0) & (slot_number < micro_count)
        slot_index = jnp.clip(slot_number, 0, micro_count - 1)
        entering = jnp.where(section_index == 0, pick_row(first_inputs, slot_index), arrived)
        modulation_row = pick_row(modulations, slot_index)
        leaving = lax.cond(
            active,
            lambda: run_forward(entering.astype(F32), modulation_row),
            lambda: jnp.zeros((length, features), F32),
        ).astype(BF16)
        stored = put_slot(stored, slot_index, active, entering)
        states = put_slot(states, slot_index, active, leaving)
        arrived = shifted(leaving, "section", 1)
        return (arrived, stored, states)

    forward_start = (
        jnp.zeros((length, features), BF16),
        jnp.zeros(tokens.shape, BF16),
        jnp.zeros(tokens.shape, BF16),
    )
    arrived_last, stored, states = lax.fori_loop(0, tick_count, forward_tick, forward_start)
    totals_start = empty_grads(section_params)

    def backward_tick(tick_number, carried):
        arrived, totals, stream, table_total, embed_total = carried
        slot_number = tick_number - (sections - 1 - section_index)
        active = (slot_number >= 0) & (slot_number < micro_count)
        slot_index = jnp.clip(slot_number, 0, micro_count - 1)
        upstream = jnp.where(
            section_index == sections - 1, pick_row(cotangent, slot_index), arrived
        ).astype(F32)
        entering = pick_row(stored, slot_index).astype(F32)
        modulation_row = pick_row(modulations, slot_index)
        condition_row = pick_row(conditions, slot_index)
        grad_current, grad_modulation, tick_terms = lax.cond(
            active,
            lambda: run_backward(entering, upstream, modulation_row, condition_row),
            lambda: (
                jnp.zeros((length, features), F32),
                jnp.zeros((3 * features,), F32),
                empty_grads(section_params),
            ),
        )
        mask_row = pick_row(in_span, slot_index) & (section_index == 0)
        embed_total = embed_total + jnp.sum(jnp.where(mask_row[:, None], grad_current, 0.0), 0)
        grad_condition = jnp.dot(mod_weight[0], grad_modulation, precision=HIGH)
        silu_pull = jax.vjp(jax.nn.silu, pick_row(embedded, slot_index))[1]
        grad_embedded = silu_pull(grad_condition)[0]
        table_total = (
            table_total + pick_row(step_onehot, slot_index)[:, None] * grad_embedded[None, :]
        )
        totals = jax.tree.map(jnp.add, totals, tick_terms)
        leaving = jnp.where(mask_row[:, None], 0.0, grad_current).astype(BF16)
        stream = put_slot(stream, slot_index, active, leaving)
        arrived = shifted(leaving, "section", -1)
        return (arrived, totals, stream, table_total, embed_total)

    backward_start = (
        jnp.zeros((length, features), BF16),
        totals_start,
        jnp.zeros(tokens.shape, BF16),
        jnp.zeros(time_table.shape, F32),
        jnp.zeros((features,), F32),
    )
    arrived_first, totals, stream, table_total, embed_total = lax.fori_loop(
        0, tick_count, backward_tick, backward_start
    )
    totals = lax.psum(totals, "dp")
    table_total, embed_total = lax.psum((table_total, embed_total), ("dp", "section"))
    return (
        states[None],
        stream[None],
        table_total,
        embed_total,
        totals[0][None],
        totals[1][None],
        totals[2][None],
        totals[3][None],
        totals[4][None],
        totals[5][None],
        totals[6][None],
    )


def solution(mesh):
    placed = (
        P("dp", None, None),
        P("dp"),
        P("dp"),
        P("dp"),
        P(),
        P(),
        P("section", None, None),
        P("section", None),
        P("section", None),
        P("section", None, None),
        P("section", None),
        P("section", None, None),
        P("section", None),
        P("dp", None, None),
    )
    return jax.shard_map(
        shards,
        mesh=mesh,
        in_specs=placed,
        out_specs=(
            P("section", "dp", None, None),
            P("section", "dp", None, None),
            P(),
            P(),
            P("section", None, None),
            P("section", None),
            P("section", None),
            P("section", None, None),
            P("section", None),
            P("section", None, None),
            P("section", None),
        ),
        check_vma=False,
    )
```

profile of v0, /device:TPU:0, one launch (start us, length us, event | category | flops | bytes accessed | tf_op | source)
XLA Modules:
  0.0 2200.8 jit_solution(10372808146398210864)
XLA Ops:
  20.9 508.3 %while.54 = (s32[]{:T(128)}, bf16[1024,768]{1,0:T(8,128)(2,1)}, bf16[2,1024,768]{2,1,0:T(8,128)(2,1)S(1)}, bf16[2,1024,768]{2,1,0:T(8,128)(2,1)}, s32[]{:T(128)}...) while((s32[]{:T(128)}, bf16[1024,768]{1,0:T(8,128)(2,1)}, ...), condition=%wide.region_13.14_spmd, body=%wide.region_0.13_spmd.sunk | while | flops 9709291520 | bytes 313737152 | solution.py:370
  26.4 88.3 %conditional.7 = (bf16[1024,768]{1,0:T(8,128)(2,1)}) conditional(s32[]{:T(128)} %convert_element_type.245, () %tuple.175, (pred[]{:T(512)}, f32[2,2304]{1,0:T(2,128)S(1)}, s32[]{:T(128)}, bf16[1024,768]{1,0:T(8,128)(2,1)}, f32[1,768]{1,0:T(1,128)S(1)}, /*index=5*/bf16[768,3072]{1,0:T(8,128)(2,1)}, f32[1,3072]{1,0:T(1,128)}, ...), branch_computations={%region_1.1_spmd, %region_2.12_spmd} | conditional | flops 9706932224 | bytes 225656288 | solution.py:355
  28.1 82.0 %conditional = (f32[1024,768]{1,0:T(8,128)S(1)}, f32[1024,768]{1,0:T(8,128)}, f32[1024,768]{1,0:T(8,128)}, f32[2304]{0:T(1024)S(1)}) conditional(s32[]{:T(128)} %convert_element_type.132, (f32[1024,768]{1,0:T(8,128)S(1)}, f32[1,768]{1,0:T(1,128)S(1)}, f32[2304]{0:T(1024)S(1)}, bf16[768,3072]{1,0:T(8,128)(2,1)}, f32[1,3072]{1,0:T(1,128)}, ...), branch_computations={%region_3.4_spmd, %region_6.11_spmd} | conditional | flops 9703000064 | bytes 209899872 | solution.py:332
  121.7 29.1 %collective-permute-done = bf16[1024,768]{1,0:T(8,128)(2,1)} collective-permute-done((bf16[1024,768]{1,0:T(8,128)(2,1)}, bf16[1024,768]{1,0:T(8,128)(2,1)}, u32[]{:S(2)}, u32[]{:S(2)}) %collective-permute-start) | collective-permute-done | bytes 1572896 | tf_op jit(solution)/shard_map/while/body/eval_jaxpr/ppermute | solution.py:21
  156.4 88.3 %conditional.7 = (bf16[1024,768]{1,0:T(8,128)(2,1)}) conditional(s32[]{:T(128)} %convert_element_type.245, () %tuple.175, (pred[]{:T(512)}, f32[2,2304]{1,0:T(2,128)S(1)}, s32[]{:T(128)}, bf16[1024,768]{1,0:T(8,128)(2,1)}, f32[1,768]{1,0:T(1,128)S(1)}, /*index=5*/bf16[768,3072]{1,0:T(8,128)(2,1)}, f32[1,3072]{1,0:T(1,128)}, ...), branch_computations={%region_1.1_spmd, %region_2.12_spmd} | conditional | flops 9706932224 | bytes 225656288 | solution.py:355
  158.1 82.0 %conditional = (f32[1024,768]{1,0:T(8,128)S(1)}, f32[1024,768]{1,0:T(8,128)}, f32[1024,768]{1,0:T(8,128)}, f32[2304]{0:T(1024)S(1)}) conditional(s32[]{:T(128)} %convert_element_type.132, (f32[1024,768]{1,0:T(8,128)S(1)}, f32[1,768]{1,0:T(1,128)S(1)}, f32[2304]{0:T(1024)S(1)}, bf16[768,3072]{1,0:T(8,128)(2,1)}, f32[1,3072]{1,0:T(1,128)}, ...), branch_computations={%region_3.4_spmd, %region_6.11_spmd} | conditional | flops 9703000064 | bytes 209899872 | solution.py:332
  251.7 28.6 %collective-permute-done = bf16[1024,768]{1,0:T(8,128)(2,1)} collective-permute-done((bf16[1024,768]{1,0:T(8,128)(2,1)}, bf16[1024,768]{1,0:T(8,128)(2,1)}, u32[]{:S(2)}, u32[]{:S(2)}) %collective-permute-start) | collective-permute-done | bytes 1572896 | tf_op jit(solution)/shard_map/while/body/eval_jaxpr/ppermute | solution.py:21
  287.0 31.5 %collective-permute-start = (bf16[1024,768]{1,0:T(8,128)(2,1)}, bf16[1024,768]{1,0:T(8,128)(2,1)}, u32[]{:S(2)}, u32[]{:S(2)}) collective-permute-start(bf16[1024,768]{1,0:T(8,128)(2,1)} %get-tuple-element.2044), channel_id=1, source_target_pairs={{0,1},{1,2},{2,3},{4,5},{5,6},{6,7},{8,9},{9,10},{10,11},{12,13},{... | collective-permute-start | bytes 4718600 | tf_op jit(solution)/shard_map/while/body/eval_jaxpr/ppermute | solution.py:21
  321.5 29.3 %collective-permute-done = bf16[1024,768]{1,0:T(8,128)(2,1)} collective-permute-done((bf16[1024,768]{1,0:T(8,128)(2,1)}, bf16[1024,768]{1,0:T(8,128)(2,1)}, u32[]{:S(2)}, u32[]{:S(2)}) %collective-permute-start) | collective-permute-done | bytes 1572896 | tf_op jit(solution)/shard_map/while/body/eval_jaxpr/ppermute | solution.py:21
  369.6 28.4 %collective-permute-done = bf16[1024,768]{1,0:T(8,128)(2,1)} collective-permute-done((bf16[1024,768]{1,0:T(8,128)(2,1)}, bf16[1024,768]{1,0:T(8,128)(2,1)}, u32[]{:S(2)}, u32[]{:S(2)}) %collective-permute-start) | collective-permute-done | bytes 1572896 | tf_op jit(solution)/shard_map/while/body/eval_jaxpr/ppermute | solution.py:21
  404.7 94.0 %collective-permute-start = (bf16[1024,768]{1,0:T(8,128)(2,1)}, bf16[1024,768]{1,0:T(8,128)(2,1)}, u32[]{:S(2)}, u32[]{:S(2)}) collective-permute-start(bf16[1024,768]{1,0:T(8,128)(2,1)} %get-tuple-element.2044), channel_id=1, source_target_pairs={{0,1},{1,2},{2,3},{4,5},{5,6},{6,7},{8,9},{9,10},{10,11},{12,13},{... | collective-permute-start | bytes 4718600 | tf_op jit(solution)/shard_map/while/body/eval_jaxpr/ppermute | solution.py:21
  501.7 27.4 %collective-permute-done = bf16[1024,768]{1,0:T(8,128)(2,1)} collective-permute-done((bf16[1024,768]{1,0:T(8,128)(2,1)}, bf16[1024,768]{1,0:T(8,128)(2,1)}, u32[]{:S(2)}, u32[]{:S(2)}) %collective-permute-start) | collective-permute-done | bytes 1572896 | tf_op jit(solution)/shard_map/while/body/eval_jaxpr/ppermute | solution.py:21
  532.3 1262.7 %while.55 = (s32[]{:T(128)}, bf16[1024,768]{1,0:T(8,128)(2,1)}, f32[128,2304]{1,0:T(8,128)}, f32[2304]{0:T(1024)}, f32[768]{0:T(1024)}, /*index=5*/f32[768,3072]...) while((s32[]{:T(128)}, bf16[1024,768]{1,0:T(8,128)(2,1)}, ...), condition=%wide.region_46.47_spmd.clone, body=%wide.region_14.46_spmd.clone.sunk | while | flops 29149808640 | bytes 997340544 | solution.py:414
  670.6 24.3 %collective-permute-done.1 = bf16[1024,768]{1,0:T(8,128)(2,1)} collective-permute-done((bf16[1024,768]{1,0:T(8,128)(2,1)}, bf16[1024,768]{1,0:T(8,128)(2,1)}, u32[]{:S(2)}, u32[]{:S(2)}) %collective-permute-start.1) | collective-permute-done | bytes 1572896 | tf_op jit(solution)/shard_map/while/body/eval_jaxpr/ppermute | solution.py:21
  756.1 398.3 %collective-permute-done.1 = bf16[1024,768]{1,0:T(8,128)(2,1)} collective-permute-done((bf16[1024,768]{1,0:T(8,128)(2,1)}, bf16[1024,768]{1,0:T(8,128)(2,1)}, u32[]{:S(2)}, u32[]{:S(2)}) %collective-permute-start.1) | collective-permute-done | bytes 1572896 | tf_op jit(solution)/shard_map/while/body/eval_jaxpr/ppermute | solution.py:21
  1162.4 271.2 %conditional.8 = (f32[1024,768]{1,0:T(8,128)}, f32[128,2304]{1,0:T(8,128)}, f32[2304]{0:T(1024)}, f32[768]{0:T(1024)}, f32[768,3072]{1,0:T(8,128)}, /*index=5*/f...) conditional(s32[]{:T(128)} %convert_element_type.247, () %tuple.180, (pred[]{:T(512)}, ...), branch_computations={%region_15.15_spmd, %region_16.44_spmd} | conditional | flops 29131307008 | bytes 854240128 | solution.py:384
  1166.5 262.4 %conditional.2 = (f32[1024,768]{1,0:T(8,128)}, f32[2304]{0:T(1024)}, f32[128,2304]{1,0:T(8,128)}, f32[768]{0:T(1024)}, f32[768,3072]{1,0:T(8,128)}, /*index=5*/f...) conditional(s32[]{:T(128)} %convert_element_type.153, (f32[1024,768]{1,0:T(8,128)S(1)}, ...), branch_computations={%region_17.26_spmd.clone, %region_28.43_spmd.clone} | conditional | flops 29130520576 | bytes 836875840 | solution.py:337
  1482.5 271.3 %conditional.8 = (f32[1024,768]{1,0:T(8,128)}, f32[128,2304]{1,0:T(8,128)}, f32[2304]{0:T(1024)}, f32[768]{0:T(1024)}, f32[768,3072]{1,0:T(8,128)}, /*index=5*/f...) conditional(s32[]{:T(128)} %convert_element_type.247, () %tuple.180, (pred[]{:T(512)}, ...), branch_computations={%region_15.15_spmd, %region_16.44_spmd} | conditional | flops 29131307008 | bytes 854240128 | solution.py:384
  1486.5 262.3 %conditional.2 = (f32[1024,768]{1,0:T(8,128)}, f32[2304]{0:T(1024)}, f32[128,2304]{1,0:T(8,128)}, f32[768]{0:T(1024)}, f32[768,3072]{1,0:T(8,128)}, /*index=5*/f...) conditional(s32[]{:T(128)} %convert_element_type.153, (f32[1024,768]{1,0:T(8,128)S(1)}, ...), branch_computations={%region_17.26_spmd.clone, %region_28.43_spmd.clone} | conditional | flops 29130520576 | bytes 836875840 | solution.py:337
  1577.9 22.2 %multiply_convert_fusion.2 = bf16[12,512,1024]{2,1,0:T(8,128)(2,1)} fusion(f32[12,512,1024]{2,1,0:T(8,128)} %get-tuple-element.1524, f32[12,512]{1,0:T(8,128)S(1)} %get-tuple-element.1523, f32[12,512,1024]{2,1,0:T(8,128)} %get-tuple-element.1520, f32[12,512]{1,0:T(8,128)S(1)} %get-tuple-element.1519), kind=kLoop, calls=%fused_computation.122 | loop fusion | flops 25165824 | bytes 62963712 | tf_op jit(solution)/shard_map/while/body/eval_jaxpr/cond/branch_1_fun/cond/branch_1_fun/convert_element_type | solution.py:187
  1795.9 40.5 %psum.64 = f32[768]{0:T(1024)} all-reduce(f32[768]{0:T(1024)S(1)} %copy-done.68), channel_id=1, replica_groups=mesh['dp'=8,'section'=4] {'dp','section'}, use_global_device_ids=true, to_apply=%region_48.49 | all-reduce | flops 768 | bytes 6144 | tf_op jit(solution)/shard_map/psum | solution.py:418
  1836.4 24.0 %all-reduce = (f32[1,2304]{1,0:T(1,128)}, f32[1,768]{1,0:T(1,128)}, f32[1,3072]{1,0:T(1,128)}, f32[1,768]{1,0:T(1,128)}) all-reduce(f32[1,2304]{1,0:T(1,128)S(1)} %broadcast_in_dim.184, f32[1,768]{1,0:T(1,128)S(1)} %broadcast_in_dim.185, f32[1,3072]{1,0:T(1,128)S(1)} %bitcast.198, ...), channel_id=1, replica_groups=mesh['dp'=8,'section'=4] {'dp'}, use_global_device_ids=true, to_apply=%region_50.51 | all-reduce | flops 6912 | bytes 55296 | tf_op jit(solution)/shard_map/psum | solution.py:417
  1860.3 58.5 %all-reduce.5.cloned.1.call-done = f32[512,128]{1,0:T(8,128)} async-done(((f32[512,128]{1,0:T(8,128)}), f32[512,128]{1,0:T(8,128)}) %all-reduce.5.cloned.1.call-update) | async-done | bytes 262160 | tf_op jit(solution)/shard_map/psum | solution.py:418
  1918.8 258.0 %all-reduce.7.cloned.1.call-done = (f32[1,128,2304]{2,1,0:T(8,128)}, f32[1,768,3072]{2,1,0:T(8,128)}, f32[1,3072,768]{2,1,0:T(8,128)}) async-done(((f32[1,128,2304]{2,1,0:T(8,128)}, f32[1,768,3072]{2,1,0:T(8,128)}, f32[1,3072,768]{2,1,0:T(8,128)}), (f32[1,128,2304]{2,1,0:T(8,128)}, f32[1,768,3072]{2,1,0:T(8,128)}, f32[1,3072,768]{2,1,0:T(8,128)})) %all-reduce.7.cloned.1.call-update) | async-done | bytes 20054032 | tf_op jit(solution)/shard_map/psum | solution.py:417
  (856 shorter events, 1103.4 us)
Async XLA Ops:
  7.2 1911.6 %all-reduce.5.cloned.1.call-start = ((), (), s32[]{:S(2)}) async-start(), calls=%async_computation | async-start | bytes 524288 | tf_op jit(solution)/shard_map/psum | solution.py:418
  114.7 36.1 %collective-permute-start = (bf16[1024,768]{1,0:T(8,128)(2,1)}, bf16[1024,768]{1,0:T(8,128)(2,1)}, u32[]{:S(2)}, u32[]{:S(2)}) collective-permute-start(bf16[1024,768]{1,0:T(8,128)(2,1)} %get-tuple-element.2044), channel_id=1, source_target_pairs={{0,1},{1,2},{2,3},{4,5},{5,6},{6,7},{8,9},{9,10},{10,11},{12,13},{... | collective-permute-start | bytes 4718600 | tf_op jit(solution)/shard_map/while/body/eval_jaxpr/ppermute | solution.py:21
  119.6 31.3 %copy-start.14 = (bf16[2,1024,768]{2,1,0:T(8,128)(2,1)S(1)}, bf16[2,1024,768]{2,1,0:T(8,128)(2,1)}, u32[]{:S(2)}) copy-start(bf16[2,1024,768]{2,1,0:T(8,128)(2,1)} %copy-done.13) | copy-start | bytes 9437188 | tf_op jit(solution)/shard_map/while
  244.7 35.6 %collective-permute-start = (bf16[1024,768]{1,0:T(8,128)(2,1)}, bf16[1024,768]{1,0:T(8,128)(2,1)}, u32[]{:S(2)}, u32[]{:S(2)}) collective-permute-start(bf16[1024,768]{1,0:T(8,128)(2,1)} %get-tuple-element.2044), channel_id=1, source_target_pairs={{0,1},{1,2},{2,3},{4,5},{5,6},{6,7},{8,9},{9,10},{10,11},{12,13},{... | collective-permute-start | bytes 4718600 | tf_op jit(solution)/shard_map/while/body/eval_jaxpr/ppermute | solution.py:21
  249.5 30.7 %copy-start.14 = (bf16[2,1024,768]{2,1,0:T(8,128)(2,1)S(1)}, bf16[2,1024,768]{2,1,0:T(8,128)(2,1)}, u32[]{:S(2)}) copy-start(bf16[2,1024,768]{2,1,0:T(8,128)(2,1)} %copy-done.13) | copy-start | bytes 9437188 | tf_op jit(solution)/shard_map/while
  287.0 63.8 %collective-permute-start = (bf16[1024,768]{1,0:T(8,128)(2,1)}, bf16[1024,768]{1,0:T(8,128)(2,1)}, u32[]{:S(2)}, u32[]{:S(2)}) collective-permute-start(bf16[1024,768]{1,0:T(8,128)(2,1)} %get-tuple-element.2044), channel_id=1, source_target_pairs={{0,1},{1,2},{2,3},{4,5},{5,6},{6,7},{8,9},{9,10},{10,11},{12,13},{... | collective-permute-start | bytes 4718600 | tf_op jit(solution)/shard_map/while/body/eval_jaxpr/ppermute | solution.py:21
  320.9 29.9 %copy-start.14 = (bf16[2,1024,768]{2,1,0:T(8,128)(2,1)S(1)}, bf16[2,1024,768]{2,1,0:T(8,128)(2,1)}, u32[]{:S(2)}) copy-start(bf16[2,1024,768]{2,1,0:T(8,128)(2,1)} %copy-done.13) | copy-start | bytes 9437188 | tf_op jit(solution)/shard_map/while
  357.6 40.3 %collective-permute-start = (bf16[1024,768]{1,0:T(8,128)(2,1)}, bf16[1024,768]{1,0:T(8,128)(2,1)}, u32[]{:S(2)}, u32[]{:S(2)}) collective-permute-start(bf16[1024,768]{1,0:T(8,128)(2,1)} %get-tuple-element.2044), channel_id=1, source_target_pairs={{0,1},{1,2},{2,3},{4,5},{5,6},{6,7},{8,9},{9,10},{10,11},{12,13},{... | collective-permute-start | bytes 4718600 | tf_op jit(solution)/shard_map/while/body/eval_jaxpr/ppermute | solution.py:21
  404.7 124.4 %collective-permute-start = (bf16[1024,768]{1,0:T(8,128)(2,1)}, bf16[1024,768]{1,0:T(8,128)(2,1)}, u32[]{:S(2)}, u32[]{:S(2)}) collective-permute-start(bf16[1024,768]{1,0:T(8,128)(2,1)} %get-tuple-element.2044), channel_id=1, source_target_pairs={{0,1},{1,2},{2,3},{4,5},{5,6},{6,7},{8,9},{9,10},{10,11},{12,13},{... | collective-permute-start | bytes 4718600 | tf_op jit(solution)/shard_map/while/body/eval_jaxpr/ppermute | solution.py:21
  573.4 36.0 %collective-permute-start.1 = (bf16[1024,768]{1,0:T(8,128)(2,1)}, bf16[1024,768]{1,0:T(8,128)(2,1)}, u32[]{:S(2)}, u32[]{:S(2)}) collective-permute-start(bf16[1024,768]{1,0:T(8,128)(2,1)} %get-tuple-element.1823), channel_id=1, source_target_pairs={{1,0},{2,1},{3,2},{5,4},{6,5},{7,6},{9,8},{10,9},{11,10},{13,12},{... | collective-permute-start | bytes 4718600 | tf_op jit(solution)/shard_map/while/body/eval_jaxpr/ppermute | solution.py:21
  636.3 58.5 %collective-permute-start.1 = (bf16[1024,768]{1,0:T(8,128)(2,1)}, bf16[1024,768]{1,0:T(8,128)(2,1)}, u32[]{:S(2)}, u32[]{:S(2)}) collective-permute-start(bf16[1024,768]{1,0:T(8,128)(2,1)} %get-tuple-element.1823), channel_id=1, source_target_pairs={{1,0},{2,1},{3,2},{5,4},{6,5},{7,6},{9,8},{10,9},{11,10},{13,12},{... | collective-permute-start | bytes 4718600 | tf_op jit(solution)/shard_map/while/body/eval_jaxpr/ppermute | solution.py:21
  659.1 35.8 %copy-start.16 = (bf16[2,1024,768]{2,1,0:T(8,128)(2,1)S(1)}, bf16[2,1024,768]{2,1,0:T(8,128)(2,1)}, u32[]{:S(2)}) copy-start(bf16[2,1024,768]{2,1,0:T(8,128)(2,1)} %copy-done.15) | copy-start | bytes 9437188 | tf_op jit(solution)/shard_map/while
  659.1 35.8 %copy-start.42 = (f32[1,768]{1,0:T(1,128)S(1)}, f32[1,768]{1,0:T(1,128)}, u32[]{:S(2)}) copy-start(f32[1,768]{1,0:T(1,128)} %copy-done.41) | copy-start | bytes 9220 | tf_op jit(solution)/shard_map/while
  659.1 35.8 %copy-start.65 = (pred[2,1024]{1,0:T(4,128)(4,1)S(1)}, pred[2,1024]{1,0:T(4,128)(4,1)}, u32[]{:S(2)}) copy-start(pred[2,1024]{1,0:T(4,128)(4,1)} %get-tuple-element.2096) | copy-start | bytes 6148 | tf_op jit(solution)/shard_map/while
  721.8 432.5 %collective-permute-start.1 = (bf16[1024,768]{1,0:T(8,128)(2,1)}, bf16[1024,768]{1,0:T(8,128)(2,1)}, u32[]{:S(2)}, u32[]{:S(2)}) collective-permute-start(bf16[1024,768]{1,0:T(8,128)(2,1)} %get-tuple-element.1823), channel_id=1, source_target_pairs={{1,0},{2,1},{3,2},{5,4},{6,5},{7,6},{9,8},{10,9},{11,10},{13,12},{... | collective-permute-start | bytes 4718600 | tf_op jit(solution)/shard_map/while/body/eval_jaxpr/ppermute | solution.py:21
  744.6 409.8 %copy-start.16 = (bf16[2,1024,768]{2,1,0:T(8,128)(2,1)S(1)}, bf16[2,1024,768]{2,1,0:T(8,128)(2,1)}, u32[]{:S(2)}) copy-start(bf16[2,1024,768]{2,1,0:T(8,128)(2,1)} %copy-done.15) | copy-start | bytes 9437188 | tf_op jit(solution)/shard_map/while
  744.6 409.8 %copy-start.42 = (f32[1,768]{1,0:T(1,128)S(1)}, f32[1,768]{1,0:T(1,128)}, u32[]{:S(2)}) copy-start(f32[1,768]{1,0:T(1,128)} %copy-done.41) | copy-start | bytes 9220 | tf_op jit(solution)/shard_map/while
  744.6 409.8 %copy-start.65 = (pred[2,1024]{1,0:T(4,128)(4,1)S(1)}, pred[2,1024]{1,0:T(4,128)(4,1)}, u32[]{:S(2)}) copy-start(pred[2,1024]{1,0:T(4,128)(4,1)} %get-tuple-element.2096) | copy-start | bytes 6148 | tf_op jit(solution)/shard_map/while
  1162.4 271.2 %copy-start.62 = (pred[1024]{0:T(1024)(128)(4,1)S(1)}, pred[1024]{0:T(1024)(128)(4,1)}, u32[]{:S(2)}) copy-start(pred[1024]{0:T(1024)(128)(4,1)} %and_reduce_fusion.2) | copy-start | bytes 3076 | tf_op jit(solution)/shard_map/while
  1438.2 36.0 %collective-permute-start.1 = (bf16[1024,768]{1,0:T(8,128)(2,1)}, bf16[1024,768]{1,0:T(8,128)(2,1)}, u32[]{:S(2)}, u32[]{:S(2)}) collective-permute-start(bf16[1024,768]{1,0:T(8,128)(2,1)} %get-tuple-element.1823), channel_id=1, source_target_pairs={{1,0},{2,1},{3,2},{5,4},{6,5},{7,6},{9,8},{10,9},{11,10},{13,12},{... | collective-permute-start | bytes 4718600 | tf_op jit(solution)/shard_map/while/body/eval_jaxpr/ppermute | solution.py:21
  1482.5 271.4 %copy-start.62 = (pred[1024]{0:T(1024)(128)(4,1)S(1)}, pred[1024]{0:T(1024)(128)(4,1)}, u32[]{:S(2)}) copy-start(pred[1024]{0:T(1024)(128)(4,1)} %and_reduce_fusion.2) | copy-start | bytes 3076 | tf_op jit(solution)/shard_map/while
  1758.4 34.2 %collective-permute-start.1 = (bf16[1024,768]{1,0:T(8,128)(2,1)}, bf16[1024,768]{1,0:T(8,128)(2,1)}, u32[]{:S(2)}, u32[]{:S(2)}) collective-permute-start(bf16[1024,768]{1,0:T(8,128)(2,1)} %get-tuple-element.1823), channel_id=1, source_target_pairs={{1,0},{2,1},{3,2},{5,4},{6,5},{7,6},{9,8},{10,9},{11,10},{13,12},{... | collective-permute-start | bytes 4718600 | tf_op jit(solution)/shard_map/while/body/eval_jaxpr/ppermute | solution.py:21
  1795.1 381.8 %all-reduce.7.cloned.1.call-start = ((), (), s32[]{:S(2)}) async-start(), calls=%async_computation.1 | async-start | bytes 40108032 | tf_op jit(solution)/shard_map/psum | solution.py:417
  1795.2 41.2 %copy-start.50 = (f32[3072]{0:T(1024)S(1)}, f32[3072]{0:T(1024)}, u32[]{:S(2)}) copy-start(f32[3072]{0:T(1024)} %get-tuple-element.2069) | copy-start | bytes 36868
  (247 other events, 2185.9 us)
Sparse Core Ops, SparseCore 0:
  1795.2 123.5 all-reduce.4
  1924.3 252.5 all-reduce.6
where the time goes:
time: 2230 us; the launch traced here: 2200 us
  waiting for transfers between devices  891 us (40%)
  matrix products  452 us (20%)
  other arithmetic  384 us (17%)
  local copies, waits for them, and re-layouts  207 us (9%)
  starting transfers between devices  147 us (7%)
  blocking collectives  64.4 us (3%)
  loops' own time  40.4 us (2%)
    ppermute x10, waiting for transfers between devices, shifted(): lax.ppermute(value, axis, [(source, source + steps) for source in range(f...  574 us
    psum x1, waiting for transfers between devices, shards(): totals = lax.psum(totals, 'dp')  258 us
    ppermute x10, starting transfers between devices, shifted(): lax.ppermute(value, axis, [(source, source + steps) for source in range(f...  147 us
    add x30, other arithmetic, backward_tick(): totals = jax.tree.map(jnp.add, totals, tick_terms)  137 us
    sub x8, matrix products, softmax_rows(): exponents = jnp.exp(scores - row_max)  104 us
    dot_general x8, matrix products, attention_mix(): jnp.einsum('hqk,khd->qhd', weights_low, value_rows, preferred_element_typ...  88.7 us
    convert_element_type x4, other arithmetic, attention_backward(): grad_scores = (weights_block * (grad_weights - row_dot)).astype(BF16)  87.2 us
    dot_general x4, matrix products, attention_backward(): jnp.einsum('qhd,khd->hqk', grad_block, value_rows, preferred_element_type...  71.3 us
  transfers between devices with their start and end apart: 12, of which 11 were waited for; matrix products, arithmetic and copies ran while one was open for 8% of the time, Pallas kernels for 0%

commit v1 on v0

v1 whole, which is shorter than its diff:
```python
from functools import partial
import math

import jax
import jax.numpy as jnp
from jax import lax
from jax.experimental import pallas as pl
from jax.experimental.pallas import tpu as pltpu
from jax.sharding import PartitionSpec as P

HEAD = 64
HALF = HEAD // 2
EPS = 1e-06
HIGH = lax.Precision.HIGHEST
F32 = jnp.float32
BF16 = jnp.bfloat16
SCALE = HEAD ** (-0.5)
EXP2_SCALE = SCALE * math.log2(math.e)
GELU_C = math.sqrt(2.0 / math.pi)
VMEM_LIMIT = 56 << 20
AXES = ("dp", "section")


def dot_nn(left, right):
    return jnp.dot(left, right, preferred_element_type=F32)


def dot_nt(left, right):
    return lax.dot_general(left, right, (((1,), (1,)), ((), ())), preferred_element_type=F32)


def params(**more):
    return pltpu.CompilerParams(vmem_limit_bytes=VMEM_LIMIT, **more)


def shape(dims, dtype):
    return jax.ShapeDtypeStruct(dims, dtype)


def normalize(rows):
    average = jnp.mean(rows, -1, keepdims=True)
    centered = rows - average
    inverse_std = lax.rsqrt(jnp.mean(centered * centered, -1, keepdims=True) + EPS)
    return centered * inverse_std, inverse_std


MESH = pl.DeviceIdType.MESH
CHUNKS = 2


def pipeline_kernel(
    enter_ref, cot_ref, wide_ref, second_ref, mods_ref, gain_ref, keep_ref, bias_column_ref, bias_row_ref,
    out_bias_ref, cos_ref, sin_ref,
    states_ref, stream_ref, kept_first, kept_second, kept_rows, back_first, back_second, sums_ref,
    weights, streams, others, upstreams, up_others, mixed_got, first_buf, second_buf, branches, leaving,
    mixed_own, mixed_send, grad_send, grad_own, lse_ref,
    load_sem, pass_send, pass_recv, back_recv, swap_send, swap_recv, place_send, place_recv, store_sem, fetch_sem,
):
    section = lax.axis_index("section")
    sections = lax.axis_size("section")
    dp_index = lax.axis_index("dp")
    core = lax.rem(dp_index, 2)
    partner = dp_index + 1 - 2 * core
    micros, half, features = streams.shape
    width = mixed_own.shape[1]
    heads = width // HEAD
    length = 2 * half
    part_rows = half // CHUNKS
    attends = lax.rem(section, 2) == 0
    feeds = lax.rem(section, 2) == 1
    is_first = section == 0
    is_last = section == sections - 1
    hidden = wide_ref.shape[0]
    feed_step = half
    feed_parts = hidden // feed_step

    barrier = pltpu.get_barrier_semaphore()
    pl.semaphore_signal(barrier, inc=1, device_id=(partner, section), device_id_type=MESH)

    @pl.when(section > 0)
    def _():
        pl.semaphore_signal(barrier, inc=1, device_id=(dp_index, section - 1), device_id_type=MESH)

    @pl.when(section < sections - 1)
    def _():
        pl.semaphore_signal(barrier, inc=1, device_id=(dp_index, section + 1), device_id_type=MESH)

    def load_wide():
        return pltpu.make_async_copy(wide_ref, weights, load_sem.at[0])

    def second_at(part):
        return others.at[part] if part < micros else up_others.at[part - micros]

    def load_second(part):
        return pltpu.make_async_copy(
            second_ref.at[pl.ds(part * feed_step, feed_step)], second_at(part), load_sem.at[1 + part]
        )

    def load_enter(m):
        return pltpu.make_async_copy(enter_ref.at[m], streams.at[m], fetch_sem.at[1 + m])

    def load_cot(m):
        return pltpu.make_async_copy(cot_ref.at[m], upstreams.at[m], fetch_sem.at[1 + m])

    @pl.when(is_first)
    def _():
        for m in range(micros):
            load_enter(m).start()

    load_wide().start()

    @pl.when(feeds)
    def _():
        for part in range(feed_parts):
            load_second(part).start()

    @pl.when(is_last)
    def _():
        for m in range(micros):
            load_cot(m).start()

    load_wide().wait()

    @pl.when(feeds)
    def _():
        for part in range(feed_parts):
            load_second(part).wait()

    pl.semaphore_wait(
        barrier, 1 + jnp.where(section > 0, 1, 0) + jnp.where(section < sections - 1, 1, 0)
    )

    def rows_of(part):
        return slice(part * part_rows, (part + 1) * part_rows)

    def schedule(step):
        turns = jnp.where(is_last, 1, 0)
        forward = jnp.where(is_last, 1 - lax.rem(step, 2), jnp.where(step < micros, 1, 0))
        micro = jnp.where(is_last, step // 2, lax.rem(step, micros))
        del turns
        return forward == 1, micro

    def pass_on(step, part, micro, forward):
        slot = lax.rem(step, 2)
        source = leaving.at[slot, pl.ds(part * part_rows, part_rows)]
        if forward:
            return pltpu.make_async_remote_copy(
                source, streams.at[micro, pl.ds(part * part_rows, part_rows)],
                pass_send.at[slot, part], pass_recv.at[micro, part],
                device_id=(dp_index, section + 1), device_id_type=MESH,
            )
        return pltpu.make_async_remote_copy(
            source, upstreams.at[micro, pl.ds(part * part_rows, part_rows)],
            pass_send.at[slot, part], back_recv.at[micro, part],
            device_id=(dp_index, section - 1), device_id_type=MESH,
        )

    def place_target(target, micro):
        return target.at[micro // 2, pl.ds(core * half, half)]

    def place_local(step, micro, target):
        slot = lax.rem(step, 2)
        return pltpu.make_async_copy(leaving.at[slot], place_target(target, micro), place_send.at[slot])

    def place_remote(step, micro, target, index):
        slot = lax.rem(step, 2)
        return pltpu.make_async_remote_copy(
            leaving.at[slot], place_target(target, micro), place_send.at[slot],
            place_recv.at[index, micro // 2], device_id=(partner, section), device_id_type=MESH,
        )

    def send_part(step, part, micro, forward):
        reaches = section < sections - 1 if forward else section > 0

        @pl.when(reaches)
        def _():
            pass_on(step, part, micro, forward).start()

    def place_result(step, micro, forward):
        target, index = (states_ref, 0) if forward else (stream_ref, 1)
        mine = lax.rem(micro, 2) == core

        @pl.when(mine)
        def _():
            place_local(step, micro, target).start()

        @pl.when(jnp.logical_not(mine))
        def _():
            place_remote(step, micro, target, index).start()

    def leaving_free(step):
        was_forward, micro = schedule(step)
        mine = lax.rem(micro, 2) == core
        for forward, cond in ((True, was_forward), (False, jnp.logical_not(was_forward))):
            reaches = section < sections - 1 if forward else section > 0
            target, index = (states_ref, 0) if forward else (stream_ref, 1)

            @pl.when(cond & reaches)
            def _():
                for part in range(CHUNKS):
                    pass_on(step, part, micro, forward).wait_send()

            @pl.when(cond & mine)
            def _():
                place_local(step, micro, target).wait()

            @pl.when(cond & jnp.logical_not(mine))
            def _():
                place_remote(step, micro, target, index).wait_send()

    def swap(kind, source, target, micro):
        return pltpu.make_async_remote_copy(
            source, target, swap_send.at[kind], swap_recv.at[kind, micro],
            device_id=(partner, section), device_id_type=MESH,
        )

    def store_out(source, target, which):
        return pltpu.make_async_copy(source, target, store_sem.at[which])

    def stores_done():
        store_out(first_buf.at[0], kept_first.at[0], 0).wait()
        store_out(second_buf, kept_second.at[0], 1).wait()

    def arrive(micro, part, forward):
        local = is_first if forward else is_last

        if part == 0:

            @pl.when(local)
            def _():
                (load_enter if forward else load_cot)(micro).wait()

        @pl.when(jnp.logical_not(local))
        def _():
            pass_on(0, part, micro, forward).wait_recv()

    def attention_forward(step, micro):
        mod = mods_ref[pl.ds(micro * 8, 8), :]
        gain = gain_ref[...]
        slot = lax.rem(micro, 2)
        for part in range(CHUNKS):
            arrive(micro, part, True)
        exchange = swap(0, streams.at[micro], others.at[micro], micro)
        exchange.start()

        @pl.when(step > 0)
        def _():
            stores_done()

        def project(source, part):
            standard, _ = normalize(source[micro, rows_of(part % CHUNKS), :].astype(F32))
            rows = (standard * gain * (1.0 + mod[1:2]) + mod[0:1]).astype(BF16)
            place = (part // CHUNKS) * features
            second_buf[rows_of(part % CHUNKS), place : place + features] = rows
            projected = dot_nt(weights[: 3 * width, :], rows) + bias_column_ref[:, 0:1]
            columns = slice(part * part_rows, (part + 1) * part_rows)
            cosine = cos_ref[:, columns]
            sine = sin_ref[:, columns]
            for block in range(3):
                lanes = slice(block * length + part * part_rows, block * length + (part + 1) * part_rows)
                if block == 2:
                    first_buf[slot, :width, lanes] = projected[2 * width :].astype(BF16)
                    continue
                for head in range(heads):
                    base = block * width + head * HEAD
                    front = projected[base : base + HALF]
                    back = projected[base + HALF : base + HEAD]
                    at = head * HEAD
                    first_buf[slot, at : at + HALF, lanes] = (front * cosine - back * sine).astype(BF16)
                    first_buf[slot, at + HALF : at + HEAD, lanes] = (back * cosine + front * sine).astype(BF16)

        for part in range(CHUNKS):
            project(streams, part)
        exchange.wait_recv()
        for part in range(CHUNKS, 2 * CHUNKS):
            project(others, part)

        def scores_of(head):
            base = pl.multiple_of(head * HEAD, HEAD)
            key_rows = first_buf[slot, pl.ds(base, HEAD), length : 2 * length].T
            return dot_nn(key_rows, first_buf[slot, pl.ds(base, HEAD), :length])

        def finish(head, within, scores):
            base = pl.multiple_of(head * HEAD, HEAD)
            top = jnp.max(scores, 0, keepdims=True) * EXP2_SCALE
            spread = jnp.exp2(scores * EXP2_SCALE - top)
            total = jnp.sum(spread, 0, keepdims=True)
            mixed = dot_nn(first_buf[slot, pl.ds(base, HEAD), 2 * length :], spread.astype(BF16))
            lse_ref[micro, pl.ds(head, 1), :] = top + jnp.log2(total)
            return (mixed * (1.0 / total)).astype(BF16)

        def head_pair(pair, carried):
            scores = scores_of(2 * pair), scores_of(2 * pair + 1)
            mixed = jnp.concatenate([finish(2 * pair + i, i, scores[i]) for i in range(2)], 0)
            at = pl.multiple_of(pair * length, length)
            first_buf[slot, width:, pl.ds(at, length)] = mixed
            turned = mixed.T
            lanes = pl.multiple_of(pair * 2 * HEAD, 2 * HEAD)
            mixed_own[:, pl.ds(lanes, 2 * HEAD)] = turned[:half]
            mixed_send[:, pl.ds(lanes, 2 * HEAD)] = turned[half:]
            return carried

        lax.fori_loop(0, heads // 2, head_pair, 0)
        give = swap(1, mixed_send, mixed_got.at[micro], micro)
        give.start()
        store_out(first_buf.at[slot], kept_first.at[micro], 0).start()
        store_out(second_buf, kept_second.at[micro], 1).start()

        @pl.when(step >= 2)
        def _():
            leaving_free(step - 2)

        give.wait_recv()
        for part in range(CHUNKS):
            rows = rows_of(part)
            branch = (
                dot_nn(mixed_own[rows, :], weights[3 * width : 4 * width, :])
                + dot_nn(mixed_got[micro, rows, :], weights[4 * width : 5 * width, :])
                + bias_row_ref[:, 3 * features :]
            )
            branches[micro, rows, :] = branch.astype(BF16)
            result = streams[micro, rows, :].astype(F32) + mod[2:3] * branch
            leaving[lax.rem(step, 2), rows, :] = result.astype(BF16)
            send_part(step, part, micro, True)
        place_result(step, micro, True)
        exchange.wait_send()
        give.wait_send()

    def feed_forward(step, micro):
        mod = mods_ref[pl.ds(micro * 8, 8), :]
        gain = gain_ref[...]

        @pl.when(step > 0)
        def _():
            stores_done()

        @pl.when(step >= 2)
        def _():
            leaving_free(step - 2)

        row_store = pltpu.make_async_copy(up_others.at[2], kept_rows.at[micro], store_sem.at[2])
        for part in range(CHUNKS):
            rows = rows_of(part)
            arrive(micro, part, True)
            standard, _ = normalize(streams[micro, rows, :].astype(F32))
            entering = (standard * gain * (1.0 + mod[1:2]) + mod[0:1]).astype(BF16)
            up_others[2, rows, :] = entering
            branch = jnp.broadcast_to(out_bias_ref[...], (part_rows, features))
            for piece in range(feed_parts):
                lanes = slice(piece * feed_step, (piece + 1) * feed_step)
                value = dot_nt(entering, weights[lanes, :]) + bias_row_ref[:, lanes]
                square = value * value
                bend = jnp.tanh(GELU_C * value * (1.0 + 0.044715 * square))
                active = (0.5 * value * (1.0 + bend)).astype(BF16)
                second_buf[rows, lanes] = active
                first_buf[0, rows, lanes] = (
                    0.5 * (1.0 + bend)
                    + (0.5 * GELU_C) * value * (1.0 - bend * bend) * (1.0 + (3 * 0.044715) * square)
                ).astype(BF16)
                branch = branch + dot_nn(active, second_at(piece)[...])
            branches[micro, rows, :] = branch.astype(BF16)
            result = streams[micro, rows, :].astype(F32) + mod[2:3] * branch
            leaving[lax.rem(step, 2), rows, :] = result.astype(BF16)
            send_part(step, part, micro, True)
        place_result(step, micro, True)
        store_out(first_buf.at[0], kept_first.at[micro], 0).start()
        store_out(second_buf, kept_second.at[micro], 1).start()
        row_store.start()
        row_store.wait()

    def attention_backward(step, micro):
        mod = mods_ref[pl.ds(micro * 8, 8), :]
        gain = gain_ref[...]
        stores_done()
        fetch = pltpu.make_async_copy(kept_first.at[micro], first_buf.at[0], fetch_sem.at[0])
        fetch.start()
        for part in range(CHUNKS):
            arrive(micro, part, False)
        exchange = swap(2, upstreams.at[micro], up_others.at[micro], micro)
        exchange.start()
        grad_mixed_at = 2 * features

        def into_heads(source, part):
            grad_branch = (mod[2:3] * source[micro, rows_of(part % CHUNKS), :].astype(F32)).astype(BF16)
            place = (part // CHUNKS) * features
            second_buf[rows_of(part % CHUNKS), place : place + features] = grad_branch
            lanes = slice(grad_mixed_at + part * part_rows, grad_mixed_at + (part + 1) * part_rows)
            second_buf[:width, lanes] = dot_nt(weights[3 * width : 4 * width, :], grad_branch).astype(BF16)

        for part in range(CHUNKS):
            into_heads(upstreams, part)
        exchange.wait_recv()
        for part in range(CHUNKS, 2 * CHUNKS):
            into_heads(up_others, part)
        fetch.wait()
        cosine = cos_ref[...]
        sine = sin_ref[...]

        def turn_back(base, block, gradient):
            lanes = slice(block * length, (block + 1) * length)
            front = gradient[:HALF] * SCALE
            back = gradient[HALF:] * SCALE
            first_buf[1, pl.ds(base, HALF), lanes] = (front * cosine + back * sine).astype(BF16)
            first_buf[1, pl.ds(pl.multiple_of(base + HALF, HALF), HALF), lanes] = (
                back * cosine - front * sine
            ).astype(BF16)

        def one_head(head, mixed):
            base = pl.multiple_of(head * HEAD, HEAD)
            query = first_buf[0, pl.ds(base, HEAD), :length]
            key = first_buf[0, pl.ds(base, HEAD), length : 2 * length]
            value = first_buf[0, pl.ds(base, HEAD), 2 * length :]
            grad_mixed = second_buf[pl.ds(base, HEAD), grad_mixed_at : grad_mixed_at + length]
            delta = jnp.sum(grad_mixed.astype(F32) * mixed.astype(F32), 0, keepdims=True)
            scores = dot_nn(key.T, query)
            spread = jnp.exp2(scores * EXP2_SCALE - lse_ref[micro, pl.ds(head, 1), :])
            grad_spread = dot_nn(value.T, grad_mixed)
            grad_scores = (spread * (grad_spread - delta)).astype(BF16)
            grad_value = dot_nn(spread.astype(BF16), grad_mixed.T)
            grad_key = dot_nn(grad_scores, query.T)
            grad_query = dot_nn(key, grad_scores)
            turn_back(base, 0, grad_query)
            turn_back(base, 1, grad_key.T)
            first_buf[1, pl.ds(base, HEAD), 2 * length :] = grad_value.T.astype(BF16)

        def head_pair(pair, carried):
            at = pl.multiple_of(pair * length, length)
            mixed = first_buf[0, width:, pl.ds(at, length)]
            one_head(2 * pair, mixed[:HEAD])
            one_head(2 * pair + 1, mixed[HEAD:])
            return carried

        lax.fori_loop(0, heads // 2, head_pair, 0)

        def grad_rows_of(part):
            total = None
            for block in range(3):
                lanes = slice(block * length + part * part_rows, block * length + (part + 1) * part_rows)
                term = dot_nn(first_buf[1, :width, lanes].T, weights[block * width : (block + 1) * width, :])
                total = term if total is None else total + term
            return total

        for part in range(CHUNKS, 2 * CHUNKS):
            grad_send[rows_of(part - CHUNKS), :] = grad_rows_of(part).astype(BF16)
        give = swap(3, grad_send, others.at[micro], micro)
        give.start()
        store_out(first_buf.at[1], back_first.at[micro], 0).start()
        store_out(second_buf, back_second.at[micro], 1).start()
        for part in range(CHUNKS):
            grad_own[rows_of(part), :] = grad_rows_of(part)
        leaving_free(step - 2)
        give.wait_recv()
        for part in range(CHUNKS):
            rows = rows_of(part)
            finish_back(
                grad_own[rows, :] + others[micro, rows, :].astype(F32),
                streams[micro, rows, :].astype(F32),
                upstreams[micro, rows, :].astype(F32),
                branches[micro, rows, :].astype(F32),
                mod, gain, keep_ref[micro, rows, :] > 0.5,
                leaving, (lax.rem(step, 2), rows), sums_ref, micro, part == 0,
            )
            send_part(step, part, micro, False)
        place_result(step, micro, False)
        exchange.wait_send()
        give.wait_send()

    def feed_backward(step, micro):
        mod = mods_ref[pl.ds(micro * 8, 8), :]
        gain = gain_ref[...]
        stores_done()
        fetch = pltpu.make_async_copy(kept_first.at[micro], first_buf.at[0], fetch_sem.at[0])
        fetch.start()

        @pl.when(step >= 2)
        def _():
            leaving_free(step - 2)

        fetch.wait()
        for part in range(CHUNKS):
            rows = rows_of(part)
            arrive(micro, part, False)
            upstream = upstreams[micro, rows, :].astype(F32)
            grad_branch = (mod[2:3] * upstream).astype(BF16)
            second_buf[rows, :features] = grad_branch
            total = jnp.zeros((part_rows, features), F32)
            for piece in range(feed_parts):
                lanes = slice(piece * feed_step, (piece + 1) * feed_step)
                grad_active = dot_nt(grad_branch, second_at(piece)[...])
                grad_hidden = (grad_active * first_buf[0, rows, lanes].astype(F32)).astype(BF16)
                first_buf[1, rows, lanes] = grad_hidden
                total = total + dot_nn(grad_hidden, weights[lanes, :])
            finish_back(
                total,
                streams[micro, rows, :].astype(F32),
                upstream,
                branches[micro, rows, :].astype(F32),
                mod, gain, None,
                leaving, (lax.rem(step, 2), rows), sums_ref, micro, part == 0,
            )
            send_part(step, part, micro, False)
        place_result(step, micro, False)
        store_out(first_buf.at[1], back_first.at[micro], 0).start()
        store_out(second_buf, back_second.at[micro], 1).start()

    def one_step(step, carried):
        forward, micro = schedule(step)
        backward = jnp.logical_not(forward)

        @pl.when(attends & forward)
        def _():
            attention_forward(step, micro)

        @pl.when(attends & backward)
        def _():
            attention_backward(step, micro)

        @pl.when(feeds & forward)
        def _():
            feed_forward(step, micro)

        @pl.when(feeds & backward)
        def _():
            feed_backward(step, micro)

        return carried

    lax.fori_loop(0, 2 * micros, one_step, 0)
    stores_done()
    leaving_free(2 * micros - 2)
    leaving_free(2 * micros - 1)
    for index, target in enumerate((states_ref, stream_ref)):
        for slot in range(micros // 2):
            pltpu.make_async_remote_copy(
                leaving.at[0], target.at[slot, pl.ds((1 - core) * half, half)], place_send.at[0],
                place_recv.at[index, slot], device_id=(partner, section), device_id_type=MESH,
            ).wait_recv()


def finish_back(
    grad_rows, stream, upstream, branch, mod, gain, keep, leaving, place, sums_ref, micro, start,
):
    standard, inverse_std = normalize(stream)
    scaling = mod[1:2, :]
    grad_normed = grad_rows * (1.0 + scaling)
    grad_hat = grad_normed * gain
    grad_stream = upstream + inverse_std * (
        grad_hat
        - jnp.mean(grad_hat, -1, keepdims=True)
        - standard * jnp.mean(grad_hat * standard, -1, keepdims=True)
    )
    row_sum = lambda value: jnp.sum(value, 0, keepdims=True)
    with_standard = row_sum(grad_rows * standard)
    sums = [
        row_sum(grad_rows),
        with_standard * gain,
        row_sum(upstream * branch),
        with_standard * (1.0 + scaling),
    ]
    slot, rows = place
    if keep is None:
        sums.append(jnp.zeros_like(sums[0]))
        leaving[slot, rows, :] = grad_stream.astype(BF16)
    else:
        kept = jnp.where(keep, grad_stream, 0.0)
        sums.append(row_sum(grad_stream - kept))
        leaving[slot, rows, :] = kept.astype(BF16)
    sums = jnp.concatenate(sums + [jnp.zeros((3, sums[0].shape[1]), F32)], 0)
    if start:
        sums_ref[micro] = sums
    else:
        sums_ref[micro] += sums


def pipeline(enter, cot, wide, second, mods, gain, keep, bias_column, bias_row, out_bias, cosine, sine):
    micros, half, features = enter.shape
    length = 2 * half
    width = features // 2
    hidden = wide.shape[0]
    anywhere = pl.BlockSpec(memory_space=pl.ANY)
    inside = pl.BlockSpec(memory_space=pltpu.VMEM)
    seqs = micros // 2
    dma = pltpu.SemaphoreType.DMA
    rows = (micros, half, features)
    return pl.pallas_call(
        pipeline_kernel,
        in_specs=[anywhere] * 4 + [inside] * 8,
        out_specs=[anywhere] * 7 + [inside],
        out_shape=(
            shape((seqs, length, features), BF16),
            shape((seqs, length, features), BF16),
            shape((micros, half, hidden), BF16),
            shape((micros, half, hidden), BF16),
            shape(rows, BF16),
            shape((micros, half, hidden), BF16),
            shape((micros, half, hidden), BF16),
            shape((micros, 8, features), F32),
        ),
        scratch_shapes=[
            pltpu.VMEM((hidden, features), BF16),
            pltpu.VMEM(rows, BF16),
            pltpu.VMEM(rows, BF16),
            pltpu.VMEM(rows, BF16),
            pltpu.VMEM(rows, BF16),
            pltpu.VMEM((micros, half, width), BF16),
            pltpu.VMEM((2, half, hidden), BF16),
            pltpu.VMEM((half, hidden), BF16),
            pltpu.VMEM(rows, BF16),
            pltpu.VMEM((2, half, features), BF16),
            pltpu.VMEM((half, width), BF16),
            pltpu.VMEM((half, width), BF16),
            pltpu.VMEM((half, features), BF16),
            pltpu.VMEM((half, features), F32),
            pltpu.VMEM((micros, 8, length), F32),
            dma((1 + hidden // half,)),
            dma((2, CHUNKS)),
            dma((micros, CHUNKS)),
            dma((micros, CHUNKS)),
            dma((4,)),
            dma((4, micros)),
            dma((2,)),
            dma((2, seqs)),
            dma((3,)),
            dma((1 + micros,)),
        ],
        compiler_params=params(collective_id=0, has_side_effects=True),
        name="pipeline",
    )(enter, cot, wide, second, mods, gain, keep, bias_column, bias_row, out_bias, cosine, sine)


def rope_tables(length, core):
    half = length // 2
    place = lax.broadcasted_iota(jnp.int32, (HALF, length), 1)
    position = jnp.where(place < half, place + core * half, place - core * half).astype(F32)
    column = lax.broadcasted_iota(F32, (HALF, length), 0)
    angles = position * jnp.exp(column * (-2.0 * math.log(10000.0) / HEAD))
    return jnp.cos(angles), jnp.sin(angles)


def shards(
    tokens, span_start, span_length, time_step, time_table, mask_embed, mod_weight, mod_bias,
    norm_gain, in_weight, in_bias, out_weight, out_bias, cotangent,
):
    section = lax.axis_index("section")
    sections = lax.axis_size("section")
    dp_index = lax.axis_index("dp")
    dp_count = lax.axis_size("dp")
    core = dp_index % 2
    seqs, length, features = tokens.shape
    half = length // 2
    micro_count = 2 * seqs
    hidden = in_weight.shape[2]
    width = features // 2
    first = in_weight[0]
    second = out_weight[0]
    gain = norm_gain
    is_first = section == 0

    def flat(dp, sec):
        return dp * sections + sec

    def swap_cores(value, active):
        return lax.ppermute(
            value, AXES, [(flat(d, s), flat(d ^ 1, s)) for d in range(dp_count) for s in active]
        )

    every = list(range(sections))

    def by_owner(mine, theirs, count):
        out = []
        for i in range(count):
            out.append(jnp.where(core == 0, mine[i], theirs[i]))
            out.append(jnp.where(core == 0, theirs[i], mine[i]))
        return out

    position = lax.broadcasted_iota(jnp.int32, (seqs, length), 1)
    in_span = (position >= span_start[:, None]) & (position < (span_start + span_length)[:, None])
    start_rows = jnp.where(in_span[:, :, None], mask_embed[None, None, :], tokens)
    span_rows = in_span.astype(F32)

    def halves(array, axis):
        own = lax.dynamic_slice_in_dim(array, core * half, half, axis)
        other = lax.dynamic_slice_in_dim(array, (1 - core) * half, half, axis)
        return own, other

    step_onehot = (
        time_step[:, None] == lax.broadcasted_iota(jnp.int32, (seqs, time_table.shape[0]), 1)
    ).astype(F32)
    embedded = jnp.dot(step_onehot, time_table, precision=HIGH)
    conditions = jax.nn.silu(embedded)
    modulations = jnp.dot(conditions, mod_weight[0], precision=HIGH) + mod_bias[0]
    modulations = modulations.reshape(seqs, 3, features)
    span_own, span_other = halves(span_rows, 1)
    token_own, token_other = halves(start_rows, 1)
    cot_own, cot_other = halves(cotangent, 1)
    mods = by_owner(modulations, swap_cores(modulations, every), seqs)
    spans = by_owner(span_own, swap_cores(span_other, [0]), seqs)
    enter_rows = by_owner(
        token_own, [swap_cores(token_other[i], [0]) for i in range(seqs)], seqs
    )
    cot_rows = by_owner(cot_own, swap_cores(cot_other, [sections - 1]), seqs)

    cosine, sine = rope_tables(length, core)

    def head_columns(block, which):
        begin = block * features + which * width
        return lax.dynamic_slice_in_dim(first, begin, width, 1)

    weight_heads = jnp.concatenate([head_columns(block, core) for block in range(3)], 1).T
    bias_heads = jnp.concatenate(
        [lax.dynamic_slice_in_dim(in_bias[0], block * features + core * width, width, 0) for block in range(3)]
    )
    bias_heads = jnp.broadcast_to(bias_heads[:, None], (3 * width, 128))
    out_matrix = first[:, 3 * features :]
    out_own = lax.dynamic_slice_in_dim(out_matrix, core * width, width, 0)
    out_other = lax.dynamic_slice_in_dim(out_matrix, (1 - core) * width, width, 0)
    out_pair = jnp.concatenate([out_own, out_other], 0)
    out_row = in_bias[:, 3 * features :]

    keep = jnp.where(is_first, 1.0 - jnp.stack(spans), 1.0)[:, :, None]
    mods_rows = jnp.concatenate(
        [jnp.stack(mods), jnp.zeros((micro_count, 5, features), F32)], 1
    ).reshape(micro_count * 8, features)
    wide = lax.cond(
        section % 2 == 0,
        lambda: jnp.concatenate(
            [weight_heads, out_pair, jnp.zeros((hidden - 3 * width - 2 * width, features), BF16)], 0
        ),
        lambda: first.T,
    )
    states, stream, kept_first, kept_second, kept_rows, back_first, back_second, sums = pipeline(
        jnp.stack(enter_rows), jnp.stack(cot_rows), wide, second, mods_rows, gain, keep, bias_heads, in_bias,
        out_bias, cosine, sine,
    )
    states = states[None]
    stream = stream[None]

    mid = hidden // 2

    def attention_grads():
        rows = kept_second[:, :, : 2 * features].reshape(micro_count, half, 2, features)
        rows = rows.transpose(0, 2, 1, 3).reshape(micro_count * length, features)
        mixed = kept_first[:, width:].reshape(micro_count, half - width, 3, length)
        mixed = mixed.transpose(2, 1, 0, 3).reshape(width, micro_count * length)
        grad_branch = back_second[:, :, : 2 * features].reshape(micro_count, half, 2, features)
        grad_branch = grad_branch.transpose(0, 2, 1, 3).reshape(micro_count * length, features)
        grad_proj = back_first[:, :width].reshape(micro_count, width, 3, length)
        grad_proj = grad_proj.transpose(2, 1, 0, 3).reshape(3 * width, micro_count * length)
        own = jnp.concatenate([dot_nn(grad_proj, rows), dot_nn(mixed, grad_branch)], 0)
        zeros = jnp.zeros((mid, features), F32)
        bias_in = jnp.sum(grad_proj.astype(F32), 1).reshape(3, width)
        bias_out = jnp.sum(grad_branch.astype(F32).reshape(micro_count, 2, half, features)[:, 0], (0, 1))
        low = jnp.where(core == 0, bias_in, 0.0)
        high = jnp.where(core == 0, 0.0, bias_in)
        bias = jnp.concatenate([jnp.concatenate([low, high], 1).reshape(3 * features), bias_out])
        low_zeros = jnp.zeros((mid, features), BF16)
        return own, zeros, low_zeros, low_zeros, bias, jnp.zeros((features,), F32)

    def transposed_dot(left, right):
        return lax.dot_general(left, right, (((0,), (0,)), ((), ())), preferred_element_type=F32)

    def feed_grads():
        rows = kept_rows.reshape(micro_count * half, features)
        active = kept_second.reshape(micro_count * half, hidden)
        grad_branch = back_second[:, :, :features].reshape(micro_count * half, features)
        grad_hidden = back_first.reshape(micro_count * half, hidden)
        grad_first = transposed_dot(grad_hidden, rows)
        grad_second = transposed_dot(active, grad_branch)
        pick_half = lambda array, which: lax.dynamic_slice_in_dim(array, which * mid, mid, 0)
        return (
            pick_half(grad_first, core),
            pick_half(grad_second, core),
            pick_half(grad_first, 1 - core).astype(BF16),
            pick_half(grad_second, 1 - core).astype(BF16),
            jnp.sum(grad_hidden.astype(F32), 0),
            jnp.sum(grad_branch.astype(F32), 0),
        )

    own_first, own_second, send_first, send_second, bias_first, bias_second = lax.cond(
        section % 2 == 0, attention_grads, feed_grads
    )
    odd = [s for s in every if s % 2 == 1]
    own_first = own_first + swap_cores(send_first, odd).astype(F32)
    own_second = own_second + swap_cores(send_second, odd).astype(F32)

    bits = dp_count.bit_length() - 1
    chip_bits = list(range(1, bits))

    def swap_bit(value, bit, active):
        return lax.ppermute(
            value, AXES, [(flat(d, s), flat(d ^ (1 << bit), s)) for d in range(dp_count) for s in active]
        )

    def sum_over_chips(total, active):
        columns = total.shape[1] // 2
        results = []
        for part, order in enumerate((chip_bits, chip_bits[::-1])):
            piece = total[:, part * columns : (part + 1) * columns]
            for bit in order:
                size = piece.shape[0] // 2
                low = ((dp_index >> bit) & 1) == 0
                keep = jnp.where(low, piece[:size], piece[size:])
                send = jnp.where(low, piece[size:], piece[:size]).astype(BF16)
                piece = keep + swap_bit(send, bit, active).astype(F32)
            piece = piece.astype(BF16)
            for bit in order[::-1]:
                low = ((dp_index >> bit) & 1) == 0
                got = swap_bit(piece, bit, active)
                piece = jnp.where(
                    low, jnp.concatenate([piece, got], 0), jnp.concatenate([got, piece], 0)
                )
            results.append(piece)
        return jnp.concatenate(results, 1)

    sum_first = sum_over_chips(own_first, every)
    sum_second = sum_over_chips(own_second, odd)
    got_first = swap_cores(sum_first, every)
    got_second = swap_cores(sum_second, odd)
    low_first = jnp.where(core == 0, sum_first, got_first)
    high_first = jnp.where(core == 0, got_first, sum_first)
    low_second = jnp.where(core == 0, sum_second, got_second)
    high_second = jnp.where(core == 0, got_second, sum_second)

    def attention_whole():
        columns = []
        for block in range(3):
            for side in (low_first, high_first):
                columns.append(side[block * width : (block + 1) * width].T)
        out_rows = jnp.concatenate([low_first[3 * width :], high_first[3 * width :]], 0)
        return jnp.concatenate(columns + [out_rows], 1).astype(F32), jnp.zeros((hidden, features), F32)

    def feed_whole():
        return (
            jnp.concatenate([low_first, high_first], 0).T.astype(F32),
            jnp.concatenate([low_second, high_second], 0).astype(F32),
        )

    grad_in, grad_out = lax.cond(section % 2 == 0, attention_whole, feed_whole)

    small = jnp.concatenate(
        [sums[:, :3].reshape(-1), jnp.sum(sums[:, 3], 0), jnp.sum(sums[:, 4], 0), bias_first, bias_second]
    )
    packed = jnp.concatenate([small, time_step.astype(F32)])
    gathered = lax.all_gather(packed, "dp")
    pairs = gathered[:, : small.shape[0]].reshape(dp_count // 2, 2, -1).sum(1)
    count = micro_count * 3 * features
    grad_modulation = pairs[:, :count].reshape(dp_count // 2 * micro_count, 3 * features)
    rest = jnp.sum(pairs[:, count:], 0)
    steps_all = gathered[:, small.shape[0] :].astype(jnp.int32)
    steps_all = steps_all.reshape(dp_count // 2, 2, seqs).transpose(0, 2, 1).reshape(-1)
    onehot_all = (
        steps_all[:, None] == lax.broadcasted_iota(jnp.int32, (steps_all.shape[0], time_table.shape[0]), 1)
    ).astype(F32)
    embedded_all = jnp.dot(onehot_all, time_table, precision=HIGH)
    conditions_all, silu_pull = jax.vjp(jax.nn.silu, embedded_all)
    grad_mod_weight = jnp.dot(conditions_all.T, grad_modulation, precision=HIGH)
    grad_mod_bias = jnp.sum(grad_modulation, 0)
    grad_condition = lax.dot_general(
        grad_modulation, mod_weight[0], (((1,), (1,)), ((), ())), precision=HIGH, preferred_element_type=F32
    )
    grad_gain = rest[:features]
    embed_total = jnp.where(is_first, rest[features : 2 * features], 0.0)
    grad_bias_first = rest[2 * features : 2 * features + hidden]
    grad_bias_second = rest[2 * features + hidden :]
    across = lax.psum(jnp.concatenate([grad_condition.reshape(-1), embed_total]), "section")
    grad_condition = across[: grad_condition.size].reshape(grad_condition.shape)
    embed_total = across[grad_condition.size :]
    grad_embedded = silu_pull(grad_condition)[0]
    table_total = lax.dot_general(
        onehot_all, grad_embedded, (((0,), (0,)), ((), ())), precision=HIGH, preferred_element_type=F32
    )
    return (
        states,
        stream,
        table_total,
        embed_total,
        grad_mod_weight[None],
        grad_mod_bias[None],
        grad_gain[None],
        grad_in[None],
        grad_bias_first[None],
        grad_out[None],
        grad_bias_second[None],
    )


def solution(mesh):
    placed = (
        P("dp", None, None),
        P("dp"),
        P("dp"),
        P("dp"),
        P(),
        P(),
        P("section", None, None),
        P("section", None),
        P("section", None),
        P("section", None, None),
        P("section", None),
        P("section", None, None),
        P("section", None),
        P("dp", None, None),
    )
    return jax.shard_map(
        shards,
        mesh=mesh,
        in_specs=placed,
        out_specs=(
            P("section", "dp", None, None),
            P("section", "dp", None, None),
            P(),
            P(),
            P("section", None, None),
            P("section", None),
            P("section", None),
            P("section", None, None),
            P("section", None),
            P("section", None, None),
            P("section", None),
        ),
        check_vma=False,
    )
```

time: 2230 us -> 791 us (0.35)
  waiting for transfers between devices: 891 us -> 80.5 us
  matrix products: 452 us -> 27.9 us
  other arithmetic: 384 us -> 63.2 us
  Pallas kernels: 0 us -> 304 us
  starting transfers between devices: 147 us -> 30 us
  blocking collectives: 64.4 us -> 20.2 us
  loops' own time: 40.4 us -> 7.6 us
  local copies, waits for them, and re-layouts: 207 us -> 232 us
    ppermute x10 -> x25, waiting for transfers between devices: 574 us -> 29.9 us  [the longest x16 29.9 us: swap_bit(): lax.ppermute(value, AXES, [(flat(d, s), flat(d ^ 1 << bit, s)) for d in r...]
    dot_general x45 -> x6, matrix products: 345 us -> 27 us  [the longest x2 19 us: dot_nn(): return jnp.dot(left, right, preferred_element_type=F32)]
    psum x2 -> x0, waiting for transfers between devices: 317 us -> none  [the longest x1 258 us: shards(): totals = lax.psum(totals, 'dp')]
    pallas_call x0 -> x1, Pallas kernels: none -> 304 us  [pipeline(): pl.pallas_call(pipeline_kernel, in_specs=[anywhere] * 4 + [inside] * 8, o...]
    add x46 -> x4, other arithmetic: 146 us -> 5.51 us  [the longest x1 3.92 us: shards(): own_first = own_first + swap_cores(send_first, odd).astype(F32)]
    convert_element_type x16 -> x12, other arithmetic: 121 us -> 2.41 us  [the longest x1 0.73 us: shards(): span_rows = in_span.astype(F32)]
    ppermute x10 -> x25, starting transfers between devices: 147 us -> 30 us  [the longest x16 16.1 us: swap_bit(): lax.ppermute(value, AXES, [(flat(d, s), flat(d ^ 1 << bit, s)) for d in r...]
    sub x8 -> x0, matrix products: 104 us -> none  [softmax_rows(): exponents = jnp.exp(scores - row_max)]
  transfers between devices with their start and end apart: 12 -> 26, of which waited for: 11 -> 7; matrix products, arithmetic and copies ran while one was open for 8% -> 11% of each run, Pallas kernels for 0% -> 0%
where the time goes in v1:
time: 791 us; the launch traced here: 781 us
  Pallas kernels  304 us (38%)
  local copies, waits for them, and re-layouts  232 us (29%)
  waiting for transfers between devices  80.5 us (10%)
  other arithmetic  63.2 us (8%)
  starting transfers between devices  30 us (4%)
  matrix products  27.9 us (4%)
  blocking collectives  20.2 us (3%)
  between operations  15.6 us (2%)
    pallas_call x1, Pallas kernels, pipeline(): pl.pallas_call(pipeline_kernel, in_specs=[anywhere] * 4 + [inside] * 8, o...  304 us
    another operation x11, local copies, waits for them, and re-layouts  77.9 us
    unnamed x2, waiting for transfers between devices  50.6 us
    ppermute x16, waiting for transfers between devices, swap_bit(): lax.ppermute(value, AXES, [(flat(d, s), flat(d ^ 1 << bit, s)) for d in r...  29.9 us
    unnamed x58, local copies, waits for them, and re-layouts  26.6 us
    psum x1, blocking collectives, shards(): lax.psum(jnp.concatenate([grad_condition.reshape(-1), embed_total]), 'sec...  20.2 us
    cond x6, local copies, waits for them, and re-layouts  19.5 us
    dot_general x2, matrix products, dot_nn(): return jnp.dot(left, right, preferred_element_type=F32)  19 us
  transfers between devices with their start and end apart: 26, of which 7 were waited for; matrix products, arithmetic and copies ran while one was open for 11% of the time, Pallas kernels for 0%

profile of v1, /device:TPU:0, one launch (start us, length us, event | category | flops | bytes accessed | tf_op | source)
XLA Modules:
  0.0 780.9 jit_solution(7248859210720281212)
XLA Ops:
  32.5 8.6 %conditional.3 = (bf16[3072,768]{1,0:T(8,128)(2,1)}) conditional(s32[]{:T(128)} %convert_element_type.127, (bf16[768,3072]{1,0:T(8,128)(2,1)}) %tuple.127, (bf16[768,3072]{1,0:T(8,128)(2,1)}, pred[]{:T(512)}, s32[]{:T(128)}, s32[]{:T(128)}, s32[]{:T(128)}, /*index=5*/bf16[1152,768]{1,0:T(8,128)(2,1)S(1)}) %tuple.128), branch_computations={%region_0.1_spmd, %region_1.2_spmd} | conditional | flops 18874372 | bytes 12403279 | solution.py:724
  53.5 304.3 %pipeline.1 = (bf16[2,1024,768]{2,1,0:T(8,128)(2,1)}, bf16[2,1024,768]{2,1,0:T(8,128)(2,1)}, bf16[4,512,3072]{2,1,0:T(8,128)(2,1)}, bf16[4,512,3072]{2,1,0:T(8,1...) custom-call(bf16[4,512,768]{2,1,0:T(8,128)(2,1)} %get-tuple-element., ...), custom_call_target="tpu_custom_call" | custom-call | tf_op jit(solution)/shard_map/pipeline/pallas_call | solution.py:585
  357.7 192.1 %conditional.4 = (bf16[1536,768]{1,0:T(8,128)(2,1)}, bf16[1536,768]{1,0:T(8,128)(2,1)S(1)}, f32[3072]{0:T(1024)S(1)}, f32[768]{0:T(1024)S(1)}, f32[1536,768]{0,1:T(8,128)}, /*index=5*/f32[1536,768]{0,1:T(8,128)}) conditional(s32[]{:T(128)} %convert_element_type.127, (bf16[4,512,3072]{2,1,0:T(8,128)(2,1)}, bf16[4,512,768]{2,1,0:T(8,128)(2,1)}, ...), branch_computations={%region_4.7_spmd, %region_7.10_spmd} | conditional | flops 19343077376 | bytes 336679040 | solution.py:779
  365.0 16.7 %copy.154 = bf16[4,512,3072]{1,2,0:T(8,128)(2,1)} copy(bf16[4,512,3072]{2,1,0:T(8,128)(2,1)} %get-tuple-element.265) | data formatting | bytes 25165824 | tf_op jit(solution)/shard_map
  381.7 8.4 %slice.285 = bf16[4,384,3072]{1,2,0:T(8,128)(2,1)} slice(bf16[4,512,3072]{1,2,0:T(8,128)(2,1)} %copy.154), slice={[0:4], [0:384], [0:3072]} | slice | bytes 18874368 | tf_op jit(solution)/shard_map/cond/branch_1_fun/slice | solution.py:747
  395.1 16.7 %copy.157 = bf16[4,512,3072]{1,2,0:T(8,128)(2,1)} copy(bf16[4,512,3072]{2,1,0:T(8,128)(2,1)} %get-tuple-element.268) | data formatting | bytes 25165824 | tf_op jit(solution)/shard_map
  418.1 16.2 %copy.134 = bf16[3,384,4,1024]{3,2,1,0:T(4,128)(2,1)} copy(bf16[3,384,4,1024]{1,3,0,2:T(8,128)(2,1)} %bitcast.146) | data formatting | bytes 18874368 | tf_op jit(solution)/shard_map/cond/branch_1_fun/transpose | solution.py:748
  434.3 13.6 %copy.177 = bf16[144,8,4,1024]{3,1,2,0:T(8,128)(2,1)} copy(bf16[144,8,4,1024]{3,2,1,0:T(4,128)(2,1)} %bitcast.149) | data formatting | bytes 18874368 | tf_op jit(solution)/shard_map/cond
  448.0 16.7 %copy.155 = bf16[4,512,3072]{1,2,0:T(8,128)(2,1)} copy(bf16[4,512,3072]{2,1,0:T(8,128)(2,1)} %get-tuple-element.266) | data formatting | bytes 25165824 | tf_op jit(solution)/shard_map
  464.6 5.9 slice.288
  470.5 8.7 %copy.135 = bf16[4,2,512,768]{3,2,1,0:T(8,128)(2,1)} copy(bf16[4,2,512,768]{2,3,1,0:T(8,128)(2,1)} %bitcast.150) | data formatting | bytes 12582912 | tf_op jit(solution)/shard_map/cond/branch_1_fun/transpose | solution.py:742
  479.2 13.5 %fusion.44 = f32[1152,768]{1,0:T(8,128)} fusion(bf16[1152,4096]{1,0:T(8,128)(2,1)} %bitcast.160, bf16[4096,768]{1,0:T(8,128)(2,1)} %bitcast.162), kind=kOutput, calls=%fused_computation.167 | convolution fusion | flops 7247757312 | bytes 19267584 | tf_op jit(solution)/shard_map/cond/branch_1_fun/dot_general | solution.py:25
  492.6 8.6 %copy.137 = bf16[4,2,512,768]{3,2,1,0:T(8,128)(2,1)} copy(bf16[4,2,512,768]{2,3,1,0:T(8,128)(2,1)} %bitcast.148) | data formatting | bytes 12582912 | tf_op jit(solution)/shard_map/cond/branch_1_fun/transpose | solution.py:746
  501.2 16.7 %copy.156 = bf16[4,512,3072]{1,2,0:T(8,128)(2,1)} copy(bf16[4,512,3072]{2,1,0:T(8,128)(2,1)} %get-tuple-element.267) | data formatting | bytes 25165824 | tf_op jit(solution)/shard_map
  521.7 6.2 copy.136
  531.1 5.5 fusion.45
  539.2 6.0 copy.172
  581.4 10.3 %collective-permute-done.10 = bf16[768,384]{0,1:T(8,128)(2,1)S(1)} collective-permute-done((bf16[768,384]{0,1:T(8,128)(2,1)S(1)}, bf16[768,384]{0,1:T(8,128)(2,1)S(1)}, u32[]{:S(2)}, u32[]{:S(2)}) %collective-permute-start.10) | collective-permute-done | bytes 589856 | tf_op jit(solution)/shard_map/ppermute | solution.py:790
  616.3 7.1 collective-permute-done.9
  634.6 50.6 %all-reduce.4.cloned.1.call-done = f32[116752]{0:T(1024)} async-done(((f32[116752]{0:T(1024)}), f32[116752]{0:T(1024)}) %all-reduce.4.cloned.1.call-update) | async-done | bytes 467024
  703.8 20.2 %psum.7 = f32[2816]{0:T(1024)} all-reduce(f32[2816]{0:T(1024)} %pad_maximum_fusion.7), channel_id=1, replica_groups=mesh['dp'=8,'section'=4] {'section'}, use_global_device_ids=true, to_apply=%region_12.13 | all-reduce | flops 2816 | bytes 22528 | tf_op jit(solution)/shard_map/psum | solution.py:865
  738.5 26.3 %conditional.6 = (f32[1,3072,768]{2,1,0:T(8,128)S(1)}, f32[1,768,3072]{2,1,0:T(8,128)}) conditional(s32[]{:T(128)} %convert_element_type.127, (bf16[1536,768]{0,1:T(8,128)(2,1)}, bf16[1536,768]{0,1:T(8,128)(2,1)S(1)}, pred[]{:T(512)}, bf16[1536,768]{0,1:T(8,128)(2,1)}, bf16[1536,768]{0,1:T(8,128)(2,1)}) %tuple.48, (bf16[1536,768]{0,1:T(8,128)(2,1)}, ...), branch_computations={%region_14.15_spmd, %region_15.16_spmd} | conditional | flops 23592960 | bytes 56623148
  756.8 7.4 broadcast_in_dim.90
  764.8 6.3 copy.212
  (226 shorter events, 192.4 us)
Async XLA Ops:
  7.2 678.0 %all-reduce.4.cloned.1.call-start = ((), (), s32[]{:S(2)}) async-start(), calls=%async_computation | async-start | bytes 942080
  12.2 31.8 %collective-permute-start = (bf16[512,768]{1,0:T(8,128)(2,1)}, bf16[512,768]{1,0:T(8,128)(2,1)}, u32[]{:S(2)}, u32[]{:S(2)}) collective-permute-start(bf16[512,768]{1,0:T(8,128)(2,1)} %get-tuple-element.321), channel_id=1, source_target_pairs={{0,4},{4,0},{8,12},{12,8},{16,20},{20,16},{24,28},{28,24}} | collective-permute-start | bytes 2359304 | tf_op jit(solution)/shard_map/ppermute | solution.py:663
  14.8 29.2 %collective-permute-start.1 = (bf16[512,768]{1,0:T(8,128)(2,1)}, bf16[512,768]{1,0:T(8,128)(2,1)}, u32[]{:S(2)}, u32[]{:S(2)}) collective-permute-start(bf16[512,768]{1,0:T(8,128)(2,1)} %get-tuple-element.322), channel_id=1, source_target_pairs={{0,4},{4,0},{8,12},{12,8},{16,20},{20,16},{24,28},{28,24}} | collective-permute-start | bytes 2359304 | tf_op jit(solution)/shard_map/ppermute | solution.py:663
  18.1 28.5 %collective-permute-start.2 = (bf16[2,512,768]{2,1,0:T(8,128)(2,1)}, bf16[2,512,768]{2,1,0:T(8,128)(2,1)}, u32[]{:S(2)}, u32[]{:S(2)}) collective-permute-start(bf16[2,512,768]{2,1,0:T(8,128)(2,1)} %constant_dynamic-slice_fusion.12), channel_id=1, source_target_pairs={{3,7},{7,3},{11,15},{15,11},{19,23},{23,19},{27,31},{31,27}} | collective-permute-start | bytes 4718600 | tf_op jit(solution)/shard_map/ppermute | solution.py:663
  19.9 21.2 %collective-permute-start.4 = (f32[2,512]{1,0:T(2,128)S(1)}, f32[2,512]{1,0:T(2,128)S(1)}, u32[]{:S(2)}, u32[]{:S(2)}) collective-permute-start(f32[2,512]{1,0:T(2,128)S(1)} %constant_dynamic-slice_fusion.8), channel_id=1, source_target_pairs={{0,4},{4,0},{8,12},{12,8},{16,20},{20,16},{24,28},{28,24}} | collective-permute-start | bytes 12296 | tf_op jit(solution)/shard_map/ppermute | solution.py:663
  23.8 18.8 %collective-permute-start.3 = (f32[2,3,768]{2,1,0:T(4,128)}, f32[2,3,768]{2,1,0:T(4,128)}, u32[]{:S(2)}, u32[]{:S(2)}) collective-permute-start(f32[2,3,768]{2,1,0:T(4,128)} %reshape.285), channel_id=1, source_target_pairs={{0,4},{1,5},{2,6},{3,7},{4,0},{5,1},{6,2},{7,3},{8,12},{9,13},{10,... | collective-permute-start | bytes 55304 | tf_op jit(solution)/shard_map/ppermute | solution.py:663
  554.2 16.5 %collective-permute-start.5 = (bf16[1536,768]{0,1:T(8,128)(2,1)}, bf16[1536,768]{0,1:T(8,128)(2,1)}, u32[]{:S(2)}, u32[]{:S(2)}) collective-permute-start(bf16[1536,768]{0,1:T(8,128)(2,1)} %copy.160), channel_id=1, source_target_pairs={{1,5},{3,7},{5,1},{7,3},{9,13},{11,15},{13,9},{15,11},{17,21},{19,... | collective-permute-start | bytes 7077896 | tf_op jit(solution)/shard_map/ppermute | solution.py:663
  558.7 20.4 %collective-permute-start.15 = (bf16[1536,768]{0,1:T(8,128)(2,1)}, bf16[1536,768]{0,1:T(8,128)(2,1)S(1)}, u32[]{:S(2)}, u32[]{:S(2)}) collective-permute-start(bf16[1536,768]{0,1:T(8,128)(2,1)} %copy.162), channel_id=1, source_target_pairs={{1,5},{3,7},{5,1},{7,3},{9,13},{11,15},{13,9},{15,11},{17,21},{19,... | collective-permute-start | bytes 7077896 | tf_op jit(solution)/shard_map/ppermute | solution.py:663
  574.8 16.8 %collective-permute-start.10 = (bf16[768,384]{0,1:T(8,128)(2,1)S(1)}, bf16[768,384]{0,1:T(8,128)(2,1)S(1)}, u32[]{:S(2)}, u32[]{:S(2)}) collective-permute-start(bf16[768,384]{0,1:T(8,128)(2,1)S(1)} %get-tuple-element.307), channel_id=1, source_target_pairs={{0,16},{1,17},{2,18},{3,19},{4,20},{5,21},{6,22},{7,23},{8,24},{9,... | collective-permute-start | bytes 1769480 | tf_op jit(solution)/shard_map/ppermute | solution.py:790
  577.5 15.7 %collective-permute-start.6 = (bf16[768,384]{0,1:T(8,128)(2,1)S(1)}, bf16[768,384]{0,1:T(8,128)(2,1)S(1)}, u32[]{:S(2)}, u32[]{:S(2)}) collective-permute-start(bf16[768,384]{0,1:T(8,128)(2,1)S(1)} %get-tuple-element.306), channel_id=1, source_target_pairs={{0,8},{1,9},{2,10},{3,11},{4,12},{5,13},{6,14},{7,15},{8,0},{9,1},... | collective-permute-start | bytes 1769480 | tf_op jit(solution)/shard_map/ppermute | solution.py:790
  580.0 15.9 %collective-permute-start.16 = (bf16[768,384]{0,1:T(8,128)(2,1)S(1)}, bf16[768,384]{0,1:T(8,128)(2,1)S(1)}, u32[]{:S(2)}, u32[]{:S(2)}) collective-permute-start(bf16[768,384]{0,1:T(8,128)(2,1)S(1)} %get-tuple-element.300), channel_id=1, source_target_pairs={{1,9},{3,11},{5,13},{7,15},{9,1},{11,3},{13,5},{15,7},{17,25},{19,... | collective-permute-start | bytes 1769480 | tf_op jit(solution)/shard_map/ppermute | solution.py:790
  580.7 15.2 %collective-permute-start.20 = (bf16[768,384]{0,1:T(8,128)(2,1)S(1)}, bf16[768,384]{0,1:T(8,128)(2,1)S(1)}, u32[]{:S(2)}, u32[]{:S(2)}) collective-permute-start(bf16[768,384]{0,1:T(8,128)(2,1)S(1)} %get-tuple-element.301), channel_id=1, source_target_pairs={{1,17},{3,19},{5,21},{7,23},{9,25},{11,27},{13,29},{15,31},{17,1},... | collective-permute-start | bytes 1769480 | tf_op jit(solution)/shard_map/ppermute | solution.py:790
  593.6 8.6 %collective-permute-start.7 = (bf16[384,384]{0,1:T(8,128)(2,1)S(1)}, bf16[384,384]{0,1:T(8,128)(2,1)S(1)}, u32[]{:S(2)}, u32[]{:S(2)}) collective-permute-start(bf16[384,384]{0,1:T(8,128)(2,1)S(1)} %select_convert_fusion.7), channel_id=1, source_target_pairs={{0,16},{1,17},{2,18},{3,19},{4,20},{5,21},{6,22},{7,23},{8,24},{9,... | collective-permute-start | bytes 884744 | tf_op jit(solution)/shard_map/ppermute | solution.py:790
  594.1 8.9 %collective-permute-start.11 = (bf16[384,384]{0,1:T(8,128)(2,1)S(1)}, bf16[384,384]{0,1:T(8,128)(2,1)S(1)}, u32[]{:S(2)}, u32[]{:S(2)}) collective-permute-start(bf16[384,384]{0,1:T(8,128)(2,1)S(1)} %select_convert_fusion.6), channel_id=1, source_target_pairs={{0,8},{1,9},{2,10},{3,11},{4,12},{5,13},{6,14},{7,15},{8,0},{9,1},... | collective-permute-start | bytes 884744 | tf_op jit(solution)/shard_map/ppermute | solution.py:790
  596.4 8.2 %collective-permute-start.17 = (bf16[384,384]{0,1:T(8,128)(2,1)S(1)}, bf16[384,384]{0,1:T(8,128)(2,1)S(1)}, u32[]{:S(2)}, u32[]{:S(2)}) collective-permute-start(bf16[384,384]{0,1:T(8,128)(2,1)S(1)} %select_convert_fusion.5), channel_id=1, source_target_pairs={{1,17},{3,19},{5,21},{7,23},{9,25},{11,27},{13,29},{15,31},{17,1},... | collective-permute-start | bytes 884744 | tf_op jit(solution)/shard_map/ppermute | solution.py:790
  597.2 14.6 %collective-permute-start.21 = (bf16[384,384]{0,1:T(8,128)(2,1)S(1)}, bf16[384,384]{0,1:T(8,128)(2,1)S(1)}, u32[]{:S(2)}, u32[]{:S(2)}) collective-permute-start(bf16[384,384]{0,1:T(8,128)(2,1)S(1)} %select_convert_fusion.4), channel_id=1, source_target_pairs={{1,9},{3,11},{5,13},{7,15},{9,1},{11,3},{13,5},{15,7},{17,25},{19,... | collective-permute-start | bytes 884744 | tf_op jit(solution)/shard_map/ppermute | solution.py:790
  603.1 9.5 %collective-permute-start.12 = (bf16[384,384]{0,1:T(8,128)(2,1)S(1)}, bf16[384,384]{0,1:T(8,128)(2,1)S(1)}, u32[]{:S(2)}, u32[]{:S(2)}) collective-permute-start(bf16[384,384]{0,1:T(8,128)(2,1)S(1)} %add_convert_fusion.2), channel_id=1, source_target_pairs={{0,8},{1,9},{2,10},{3,11},{4,12},{5,13},{6,14},{7,15},{8,0},{9,1},... | collective-permute-start | bytes 884744 | tf_op jit(solution)/shard_map/ppermute | solution.py:790
  604.7 9.9 %collective-permute-start.18 = (bf16[384,384]{0,1:T(8,128)(2,1)S(1)}, bf16[384,384]{0,1:T(8,128)(2,1)S(1)}, u32[]{:S(2)}, u32[]{:S(2)}) collective-permute-start(bf16[384,384]{0,1:T(8,128)(2,1)S(1)} %add_convert_fusion.1), channel_id=1, source_target_pairs={{1,17},{3,19},{5,21},{7,23},{9,25},{11,27},{13,29},{15,31},{17,1},... | collective-permute-start | bytes 884744 | tf_op jit(solution)/shard_map/ppermute | solution.py:790
  610.2 13.2 %collective-permute-start.9 = (bf16[768,384]{0,1:T(8,128)(2,1)S(1)}, bf16[768,384]{0,1:T(8,128)(2,1)S(1)}, u32[]{:S(2)}, u32[]{:S(2)}) collective-permute-start(bf16[768,384]{0,1:T(8,128)(2,1)S(1)} %maximum_select_fusion.4), channel_id=1, source_target_pairs={{0,8},{1,9},{2,10},{3,11},{4,12},{5,13},{6,14},{7,15},{8,0},{9,1},... | collective-permute-start | bytes 1769480 | tf_op jit(solution)/shard_map/ppermute | solution.py:790
  612.7 12.8 %collective-permute-start.13 = (bf16[768,384]{0,1:T(8,128)(2,1)S(1)}, bf16[768,384]{0,1:T(8,128)(2,1)S(1)}, u32[]{:S(2)}, u32[]{:S(2)}) collective-permute-start(bf16[768,384]{0,1:T(8,128)(2,1)S(1)} %maximum_select_fusion.5), channel_id=1, source_target_pairs={{0,16},{1,17},{2,18},{3,19},{4,20},{5,21},{6,22},{7,23},{8,24},{9,... | collective-permute-start | bytes 1769480 | tf_op jit(solution)/shard_map/ppermute | solution.py:790
  614.7 11.4 %collective-permute-start.19 = (bf16[768,384]{0,1:T(8,128)(2,1)S(1)}, bf16[768,384]{0,1:T(8,128)(2,1)S(1)}, u32[]{:S(2)}, u32[]{:S(2)}) collective-permute-start(bf16[768,384]{0,1:T(8,128)(2,1)S(1)} %maximum_select_fusion.6), channel_id=1, source_target_pairs={{1,9},{3,11},{5,13},{7,15},{9,1},{11,3},{13,5},{15,7},{17,25},{19,... | collective-permute-start | bytes 1769480 | tf_op jit(solution)/shard_map/ppermute | solution.py:790
  615.6 11.3 %collective-permute-start.23 = (bf16[768,384]{0,1:T(8,128)(2,1)S(1)}, bf16[768,384]{0,1:T(8,128)(2,1)S(1)}, u32[]{:S(2)}, u32[]{:S(2)}) collective-permute-start(bf16[768,384]{0,1:T(8,128)(2,1)S(1)} %maximum_select_fusion.7), channel_id=1, source_target_pairs={{1,17},{3,19},{5,21},{7,23},{9,25},{11,27},{13,29},{15,31},{17,1},... | collective-permute-start | bytes 1769480 | tf_op jit(solution)/shard_map/ppermute | solution.py:790
  626.0 107.8 %collective-permute-start.14 = (bf16[1536,768]{0,1:T(8,128)(2,1)S(1)}, bf16[1536,768]{0,1:T(8,128)(2,1)}, u32[]{:S(2)}, u32[]{:S(2)}) collective-permute-start(bf16[1536,768]{0,1:T(8,128)(2,1)S(1)} %pad_maximum_fusion.5), channel_id=1, source_target_pairs={{0,4},{1,5},{2,6},{3,7},{4,0},{5,1},{6,2},{7,3},{8,12},{9,13},{10,... | collective-permute-start | bytes 7077896 | tf_op jit(solution)/shard_map/ppermute | solution.py:663
  628.7 109.7 %collective-permute-start.24 = (bf16[1536,768]{0,1:T(8,128)(2,1)}, bf16[1536,768]{0,1:T(8,128)(2,1)}, u32[]{:S(2)}, u32[]{:S(2)}) collective-permute-start(bf16[1536,768]{0,1:T(8,128)(2,1)} %pad_maximum_fusion.6), channel_id=1, source_target_pairs={{1,5},{3,7},{5,1},{7,3},{9,13},{11,15},{13,9},{15,11},{17,21},{19,... | collective-permute-start | bytes 7077896 | tf_op jit(solution)/shard_map/ppermute | solution.py:663
  (25 other events, 141.3 us)
Sparse Core Ops, SparseCore 0:
  634.7 50.4 all-reduce.3

commit v2 on v1

--- a/solution.py
+++ b/solution.py
@@ -51,9 +51,9 @@
 def pipeline_kernel(
     enter_ref, cot_ref, wide_ref, second_ref, mods_ref, gain_ref, keep_ref, bias_column_ref, bias_row_ref,
     out_bias_ref, cos_ref, sin_ref,
-    states_ref, stream_ref, kept_first, kept_second, kept_rows, back_first, back_second, sums_ref,
+    states_ref, stream_ref, kept_first, kept_second, kept_rows, back_first, back_second, sums_ref, bias_ref,
     weights, streams, others, upstreams, up_others, mixed_got, first_buf, second_buf, branches, leaving,
-    mixed_own, mixed_send, grad_send, grad_own, lse_ref,
+    mixed_own, mixed_send, grad_send, grad_own, lse_ref, bias_columns,
     load_sem, pass_send, pass_recv, back_recv, swap_send, swap_recv, place_send, place_recv, store_sem, fetch_sem,
 ):
     section = lax.axis_index("section")
@@ -129,6 +129,9 @@
     pl.semaphore_wait(
         barrier, 1 + jnp.where(section > 0, 1, 0) + jnp.where(section < sections - 1, 1, 0)
     )
+
+    bias_ref[...] = jnp.zeros_like(bias_ref)
+    bias_columns[...] = jnp.zeros_like(bias_columns)
 
     def rows_of(part):
         return slice(part * part_rows, (part + 1) * part_rows)
@@ -384,6 +387,8 @@
             grad_branch = (mod[2:3] * source[micro, rows_of(part % CHUNKS), :].astype(F32)).astype(BF16)
             place = (part // CHUNKS) * features
             second_buf[rows_of(part % CHUNKS), place : place + features] = grad_branch
+            if part < CHUNKS:
+                bias_ref[0:1, 3 * features :] += jnp.sum(grad_branch.astype(F32), 0, keepdims=True)
             lanes = slice(grad_mixed_at + part * part_rows, grad_mixed_at + (part + 1) * part_rows)
             second_buf[:width, lanes] = dot_nt(weights[3 * width : 4 * width, :], grad_branch).astype(BF16)
 
@@ -397,13 +402,14 @@
         sine = sin_ref[...]
 
         def turn_back(base, block, gradient):
-            lanes = slice(block * length, (block + 1) * length)
             front = gradient[:HALF] * SCALE
             back = gradient[HALF:] * SCALE
-            first_buf[1, pl.ds(base, HALF), lanes] = (front * cosine + back * sine).astype(BF16)
-            first_buf[1, pl.ds(pl.multiple_of(base + HALF, HALF), HALF), lanes] = (
-                back * cosine - front * sine
-            ).astype(BF16)
+            turned = jnp.concatenate([front * cosine + back * sine, back * cosine - front * sine], 0)
+            put_back(base, block, turned.astype(BF16))
+
+        def put_back(base, block, gradient):
+            first_buf[1, pl.ds(base, HEAD), block * length : (block + 1) * length] = gradient
+            bias_columns[block, pl.ds(base, HEAD), 0:1] += jnp.sum(gradient.astype(F32), 1, keepdims=True)
 
         def one_head(head, mixed):
             base = pl.multiple_of(head * HEAD, HEAD)
@@ -421,7 +427,7 @@
             grad_query = dot_nn(key, grad_scores)
             turn_back(base, 0, grad_query)
             turn_back(base, 1, grad_key.T)
-            first_buf[1, pl.ds(base, HEAD), 2 * length :] = grad_value.T.astype(BF16)
+            put_back(base, 2, grad_value.T.astype(BF16))
 
         def head_pair(pair, carried):
             at = pl.multiple_of(pair * length, length)
@@ -483,12 +489,14 @@
             upstream = upstreams[micro, rows, :].astype(F32)
             grad_branch = (mod[2:3] * upstream).astype(BF16)
             second_buf[rows, :features] = grad_branch
+            bias_ref[1:2, :features] += jnp.sum(grad_branch.astype(F32), 0, keepdims=True)
             total = jnp.zeros((part_rows, features), F32)
             for piece in range(feed_parts):
                 lanes = slice(piece * feed_step, (piece + 1) * feed_step)
                 grad_active = dot_nt(grad_branch, second_at(piece)[...])
                 grad_hidden = (grad_active * first_buf[0, rows, lanes].astype(F32)).astype(BF16)
                 first_buf[1, rows, lanes] = grad_hidden
+                bias_ref[0:1, lanes] += jnp.sum(grad_hidden.astype(F32), 0, keepdims=True)
                 total = total + dot_nn(grad_hidden, weights[lanes, :])
             finish_back(
                 total,
@@ -526,6 +534,13 @@
         return carried
 
     lax.fori_loop(0, 2 * micros, one_step, 0)
+
+    @pl.when(attends)
+    def _():
+        for block in range(3):
+            at = pl.multiple_of(block * features + core * width, 128)
+            bias_ref[0:1, pl.ds(at, width)] = bias_columns[block].T[0:1]
+
     stores_done()
     leaving_free(2 * micros - 2)
     leaving_free(2 * micros - 1)
@@ -585,7 +600,7 @@
     return pl.pallas_call(
         pipeline_kernel,
         in_specs=[anywhere] * 4 + [inside] * 8,
-        out_specs=[anywhere] * 7 + [inside],
+        out_specs=[anywhere] * 7 + [inside] * 2,
         out_shape=(
             shape((seqs, length, features), BF16),
             shape((seqs, length, features), BF16),
@@ -595,6 +610,7 @@
             shape((micros, half, hidden), BF16),
             shape((micros, half, hidden), BF16),
             shape((micros, 8, features), F32),
+            shape((8, hidden), F32),
         ),
         scratch_shapes=[
             pltpu.VMEM((hidden, features), BF16),
@@ -612,6 +628,7 @@
             pltpu.VMEM((half, features), BF16),
             pltpu.VMEM((half, features), F32),
             pltpu.VMEM((micros, 8, length), F32),
+            pltpu.VMEM((3, width, 128), F32),
             dma((1 + hidden // half,)),
             dma((2, CHUNKS)),
             dma((micros, CHUNKS)),
@@ -626,6 +643,481 @@
         compiler_params=params(collective_id=0, has_side_effects=True),
         name="pipeline",
     )(enter, cot, wide, second, mods, gain, keep, bias_column, bias_row, out_bias, cosine, sine)
+
+
+SMALL_ROWS = 24
+
+
+def gradient_kernel(
+    kept_first, kept_second, kept_rows, back_first, back_second, sums_ref, bias_ref, mod_weight_ref,
+    summed_first, summed_second, small_ref,
+    wide_a, wide_b, deep_a, deep_b, total_a, total_b, give, got, scatter_send, scatter_got, entry,
+    load_sem, pair_send, pair_recv, step_send, step_recv, gather_send, gather_recv, core_send, core_recv,
+    small_send, small_recv,
+):
+    section = lax.axis_index("section")
+    dp_index = lax.axis_index("dp")
+    dp_count = small_ref.shape[0]
+    core = lax.rem(dp_index, 2)
+    partner = dp_index + 1 - 2 * core
+    attends = lax.rem(section, 2) == 0
+    feeds = lax.rem(section, 2) == 1
+    micros, half, hidden = back_first.shape
+    features = kept_rows.shape[2]
+    width = features // 2
+    length = 2 * half
+    mid = hidden // 2
+    columns = features // 2
+    small_bits = dp_count.bit_length() - 1
+    bits = small_bits - 1
+
+    def bit_of(place):
+        return lax.rem(dp_index // (1 << place), 2)
+
+    def across(place):
+        return dp_index + (1 - 2 * bit_of(place)) * (1 << place)
+
+    barrier = pltpu.get_barrier_semaphore()
+    for place in range(small_bits):
+        pl.semaphore_signal(barrier, inc=1, device_id=(across(place), section), device_id_type=MESH)
+
+    def small_entry():
+        rows = [sums_ref[m, k : k + 1, :] for m in range(micros) for k in range(3)]
+        gain = sum(sums_ref[m, 3:4, :] for m in range(micros))
+        embed = sum(sums_ref[m, 4:5, :] for m in range(micros))
+        rows.append(gain)
+        rows += [bias_ref[0:1, k * features : (k + 1) * features] for k in range(hidden // features)]
+        rows.append(bias_ref[1:2, :features])
+        condition = []
+        for m in range(micros):
+            total = None
+            for k in range(3):
+                term = lax.dot_general(
+                    jnp.broadcast_to(sums_ref[m, k : k + 1, :], (8, features)),
+                    mod_weight_ref[:, k * features : (k + 1) * features],
+                    (((1,), (1,)), ((), ())), precision=HIGH, preferred_element_type=F32,
+                )
+                total = term if total is None else total + term
+            condition.append(total[0:1])
+        condition.append(jnp.zeros((1, features - micros * mod_weight_ref.shape[0]), F32))
+        rows.append(jnp.concatenate(condition, 1))
+        rows.append(embed)
+        rows.append(jnp.zeros((SMALL_ROWS - len(rows), features), F32))
+        entry[...] = jnp.concatenate(rows, 0)
+        small_ref[pl.ds(dp_index, 1)] = entry[...][None]
+
+    def small_copy(step):
+        size = 1 << step
+        start = (dp_index // size) * size
+        block = small_ref.at[pl.ds(start, size)]
+        return pltpu.make_async_remote_copy(
+            block, block, small_send.at[step], small_recv.at[step],
+            device_id=(across(step), section), device_id_type=MESH,
+        )
+
+    def small_wait(step):
+        size = 1 << step
+        start = (dp_index // size) * size + (1 - 2 * bit_of(step)) * size
+        block = small_ref.at[pl.ds(start, size)]
+        pltpu.make_async_remote_copy(
+            block, block, small_send.at[step], small_recv.at[step],
+            device_id=(across(step), section), device_id_type=MESH,
+        ).wait_recv()
+        small_copy(step).wait_send()
+
+    def loads(pairs, first_sem):
+        return [
+            pltpu.make_async_copy(source, target, load_sem.at[first_sem + i])
+            for i, (source, target) in enumerate(pairs)
+        ]
+
+    def spans(m):
+        return slice(m * half, (m + 1) * half)
+
+    def heads_rows(source, target, first_sem):
+        return loads(
+            [(source.at[m, :, pl.ds(0, 2 * features)], target.at[spans(m), :]) for m in range(micros)], first_sem
+        )
+
+    def heads_columns(block, target, first_sem):
+        pairs = []
+        for m in range(micros):
+            for side in range(2):
+                at = side * half
+                if block < 3:
+                    source = back_first.at[m, pl.ds(0, width), pl.ds(block * length + at, half)]
+                    pairs.append((source, target.at[pl.ds(side * width, width), spans(m)]))
+                    continue
+                for pair in range(3):
+                    rows = width // 3
+                    source = kept_first.at[m, pl.ds(width, rows), pl.ds(pair * length + at, half)]
+                    pairs.append((source, target.at[pl.ds(side * width + pair * rows, rows), spans(m)]))
+        return loads(pairs, first_sem)
+
+    def half_columns(source, which, target, first_sem):
+        return loads(
+            [(source.at[m, :, pl.ds(which * mid, mid)], target.at[spans(m), :]) for m in range(micros)], first_sem
+        )
+
+    totals = (total_a, total_b)
+    outputs = (summed_first, summed_second)
+
+    def place_order(part):
+        order = list(range(1, bits + 1))
+        return order if part == 0 else order[::-1]
+
+    def window(part, steps):
+        size = mid
+        start = 0
+        for place in place_order(part)[:steps]:
+            size = size // 2
+            start = start + bit_of(place) * size
+        return start, size
+
+    def lanes(part):
+        return pl.ds(part * columns, columns)
+
+    def step_copy(payload, part, step):
+        place = place_order(part)[step]
+        size = mid >> (step + 1)
+        return pltpu.make_async_remote_copy(
+            scatter_send.at[payload, part, pl.ds(mid - (mid >> step), size)],
+            scatter_got.at[payload, part, pl.ds(mid - (mid >> step), size)],
+            step_send.at[payload, part, step], step_recv.at[payload, part, step],
+            device_id=(across(place), section), device_id_type=MESH,
+        )
+
+    def scatter_start(payload, part, step):
+        place = place_order(part)[step]
+        start, _ = window(part, step)
+        size = mid >> (step + 1)
+        away = pl.multiple_of(start + (1 - bit_of(place)) * size, 16)
+        scatter_send[payload, part, pl.ds(mid - (mid >> step), size), :] = totals[payload][
+            pl.ds(away, size), part * columns : (part + 1) * columns
+        ].astype(BF16)
+        step_copy(payload, part, step).start()
+
+    def scatter_finish(payload, part, step):
+        step_copy(payload, part, step).wait()
+        start, size = window(part, step + 1)
+        rows = pl.ds(pl.multiple_of(start, 16), size)
+        cut = slice(part * columns, (part + 1) * columns)
+        value = totals[payload][rows, cut] + scatter_got[payload, part, pl.ds(mid - (mid >> step), size), :].astype(F32)
+        if step < bits - 1:
+            totals[payload][rows, cut] = value
+        else:
+            outputs[payload][core, rows, cut] = value.astype(BF16)
+
+    def gather_copy(payload, part, step, theirs):
+        place = place_order(part)[step]
+        start, size = window(part, step + 1)
+        if theirs:
+            start = start + (1 - 2 * bit_of(place)) * size
+        block = outputs[payload].at[core, pl.ds(pl.multiple_of(start, 16), size), lanes(part)]
+        return pltpu.make_async_remote_copy(
+            block, block, gather_send.at[payload, part, step], gather_recv.at[payload, part, step],
+            device_id=(across(place), section), device_id_type=MESH,
+        )
+
+    def core_copy(payload, part, step, other):
+        if step == bits:
+            start, size = window(part, bits)
+        else:
+            place = place_order(part)[step]
+            start, size = window(part, step + 1)
+            start = start + (1 - 2 * bit_of(place)) * size
+        side = 1 - core if other else core
+        block = outputs[payload].at[side, pl.ds(pl.multiple_of(start, 16), size), lanes(part)]
+        return pltpu.make_async_remote_copy(
+            block, block, core_send.at[payload, part, step], core_recv.at[payload, part, step],
+            device_id=(partner, section), device_id_type=MESH,
+        )
+
+    def tick(payload, number):
+        for part in range(2):
+            if number <= bits:
+                if number > 0:
+                    scatter_finish(payload, part, number - 1)
+                if number < bits:
+                    scatter_start(payload, part, number)
+                else:
+                    core_copy(payload, part, bits, False).start()
+                    gather_copy(payload, part, bits - 1, False).start()
+            else:
+                step = 2 * bits - number
+                gather_copy(payload, part, step, True).wait_recv()
+                core_copy(payload, part, step, False).start()
+                if step > 0:
+                    gather_copy(payload, part, step - 1, False).start()
+
+    last_tick = 2 * bits
+
+    def wind_up(payload):
+        for part in range(2):
+            for step in range(bits):
+                gather_copy(payload, part, step, False).wait_send()
+            for step in range(bits + 1):
+                core_copy(payload, part, step, False).wait_send()
+                core_copy(payload, part, step, True).wait_recv()
+
+    @pl.when(attends)
+    def _():
+        rows = heads_rows(kept_second, wide_a, 0)
+        grads = heads_rows(back_second, wide_b, micros)
+        buffers = (deep_a, deep_b)
+        per = 2 * micros
+        blocks = [
+            heads_columns(block, buffers[block % 2], 2 * micros + (block % 2) * 3 * per) for block in range(4)
+        ]
+        for copy in rows + blocks[0] + blocks[1]:
+            copy.start()
+        small_entry()
+        for copy in rows:
+            copy.wait()
+        for block in range(4):
+            for copy in blocks[block]:
+                copy.wait()
+            source = wide_a if block < 3 else wide_b
+            if block == 2:
+                for copy in grads:
+                    copy.start()
+            if block == 3:
+                for copy in grads:
+                    copy.wait()
+            deep = buffers[block % 2]
+            total_a[block * width : (block + 1) * width, :] = dot_nn(
+                deep[:width, :], source[:, :features]
+            ) + dot_nn(deep[width:, :], source[:, features:])
+            if block + 2 < 4:
+                for copy in blocks[block + 2]:
+                    copy.start()
+
+    def transposed_rows(source, first_sem, staged, target):
+        copies = loads(
+            [(source.at[m, :, pl.ds(0, features)], staged.at[m // 2, pl.ds((m % 2) * half, half)]) for m in range(micros)],
+            first_sem,
+        )
+
+        def turn():
+            for m in range(micros):
+                copies[m].wait()
+                target[:, m * half : (m + 1) * half] = staged[m // 2, (m % 2) * half : (m % 2 + 1) * half, :].T
+
+        return copies, turn
+
+    def pair_copy(payload):
+        return pltpu.make_async_remote_copy(
+            give, got.at[payload], pair_send.at[payload], pair_recv.at[payload],
+            device_id=(partner, section), device_id_type=MESH,
+        )
+
+    pieces = mid // features
+
+    def other_half(deep, wide, payload):
+        for piece in range(pieces):
+            give[piece * features : (piece + 1) * features, :] = dot_nn(
+                deep[...], wide[:, piece * features : (piece + 1) * features]
+            ).astype(BF16)
+
+    def own_half(deep, wide, payload):
+        for piece in range(pieces):
+            totals[payload][piece * features : (piece + 1) * features, :] = dot_nn(
+                deep[...], wide[:, piece * features : (piece + 1) * features]
+            )
+
+    def add_pair(payload):
+        pair_copy(payload).wait()
+        totals[payload][...] += got[payload].astype(F32)
+
+    @pl.when(feeds)
+    def _():
+        far = 1 - core
+        first_rows, first_turn = transposed_rows(kept_rows, 0, summed_first, deep_a)
+        second_rows = transposed_rows(back_second, micros, summed_second, deep_b)[0]
+        first_far = half_columns(back_first, far, wide_a, 2 * micros)
+        first_near = half_columns(back_first, core, wide_b, 3 * micros)
+        for copy in first_rows + first_far + first_near + second_rows:
+            copy.start()
+        small_entry()
+        first_turn()
+        for copy in first_far:
+            copy.wait()
+        other_half(deep_a, wide_a, 0)
+
+    pl.semaphore_wait(barrier, small_bits)
+    small_copy(0).start()
+
+    @pl.when(feeds)
+    def _():
+        far = 1 - core
+        first_near = half_columns(back_first, core, wide_b, 3 * micros)
+        second_far = half_columns(kept_second, far, wide_a, 4 * micros)
+        second_near = half_columns(kept_second, core, wide_b, 5 * micros)
+        second_turn = transposed_rows(back_second, micros, summed_second, deep_b)[1]
+        pair_copy(0).start()
+        for copy in second_far:
+            copy.start()
+        for copy in first_near:
+            copy.wait()
+        own_half(deep_a, wide_b, 0)
+        for copy in second_near:
+            copy.start()
+        second_turn()
+        add_pair(0)
+
+    tick(0, 0)
+
+    @pl.when(feeds)
+    def _():
+        far = 1 - core
+        second_far = half_columns(kept_second, far, wide_a, 4 * micros)
+        second_near = half_columns(kept_second, core, wide_b, 5 * micros)
+        for copy in second_far:
+            copy.wait()
+        other_half(deep_b, wide_a, 1)
+        pair_copy(1).start()
+        for copy in second_near:
+            copy.wait()
+        own_half(deep_b, wide_b, 1)
+        add_pair(1)
+
+    for number in range(last_tick + 2):
+        if number + 1 <= last_tick:
+            tick(0, number + 1)
+        if number <= last_tick:
+
+            @pl.when(feeds)
+            def _():
+                tick(1, number)
+
+        if number < small_bits:
+            small_wait(number)
+            if number + 1 < small_bits:
+                small_copy(number + 1).start()
+    for number in range(last_tick + 2, small_bits):
+        small_wait(number)
+        if number + 1 < small_bits:
+            small_copy(number + 1).start()
+    wind_up(0)
+
+    @pl.when(feeds)
+    def _():
+        wind_up(1)
+
+
+def summed_gradients(kept_first, kept_second, kept_rows, back_first, back_second, sums, bias, mod_weight, dp_count):
+    micros, half, hidden = back_first.shape
+    features = kept_rows.shape[2]
+    mid = hidden // 2
+    small_bits = dp_count.bit_length() - 1
+    bits = small_bits - 1
+    anywhere = pl.BlockSpec(memory_space=pl.ANY)
+    inside = pl.BlockSpec(memory_space=pltpu.VMEM)
+    dma = pltpu.SemaphoreType.DMA
+    tokens = micros * half
+    return pl.pallas_call(
+        gradient_kernel,
+        in_specs=[anywhere] * 5 + [inside] * 3,
+        out_specs=[inside] * 3,
+        out_shape=(
+            shape((2, mid, features), BF16),
+            shape((2, mid, features), BF16),
+            shape((dp_count, SMALL_ROWS, features), F32),
+        ),
+        scratch_shapes=[
+            pltpu.VMEM((tokens, mid), BF16),
+            pltpu.VMEM((tokens, mid), BF16),
+            pltpu.VMEM((features, tokens), BF16),
+            pltpu.VMEM((features, tokens), BF16),
+            pltpu.VMEM((mid, features), F32),
+            pltpu.VMEM((mid, features), F32),
+            pltpu.VMEM((mid, features), BF16),
+            pltpu.VMEM((2, mid, features), BF16),
+            pltpu.VMEM((2, 2, mid - (mid >> bits), features // 2), BF16),
+            pltpu.VMEM((2, 2, mid - (mid >> bits), features // 2), BF16),
+            pltpu.VMEM((SMALL_ROWS, features), F32),
+            dma((14 * micros,)),
+            dma((2,)),
+            dma((2,)),
+            dma((2, 2, bits)),
+            dma((2, 2, bits)),
+            dma((2, 2, bits)),
+            dma((2, 2, bits)),
+            dma((2, 2, bits + 1)),
+            dma((2, 2, bits + 1)),
+            dma((small_bits,)),
+            dma((small_bits,)),
+        ],
+        compiler_params=pltpu.CompilerParams(vmem_limit_bytes=62 << 20, collective_id=1, has_side_effects=True),
+        name="summed_gradients",
+    )(kept_first, kept_second, kept_rows, back_first, back_second, sums, bias, mod_weight)
+
+
+def place_kernel(first_ref, second_ref, small_ref, conditions_ref, grad_in, grad_out, mod_weight_grad, rows_ref):
+    step = pl.program_id(0)
+    attends = lax.rem(lax.axis_index("section"), 2) == 0
+    features = grad_in.shape[0]
+    width = features // 2
+
+    for index in range(8):
+        block, side = index // 2, index % 2
+
+        @pl.when(attends & (step == index))
+        def _():
+            if block < 3:
+                grad_in[...] = first_ref[side, block * width : (block + 1) * width, :].astype(F32).T
+            else:
+                for half in range(2):
+                    grad_in[half * width : (half + 1) * width, :] = first_ref[
+                        half, 3 * width :, side * width : (side + 1) * width
+                    ].astype(F32)
+            grad_out[...] = jnp.zeros_like(grad_out)
+
+        @pl.when(jnp.logical_not(attends) & (step == index))
+        def _():
+            owner, piece, cut = index // 4, (index % 4) // 2, index % 2
+            rows = slice(piece * features, (piece + 1) * features)
+            lanes = slice(cut * width, (cut + 1) * width)
+            grad_in[...] = first_ref[owner, rows, lanes].astype(F32)
+            grad_out[...] = second_ref[owner, rows, lanes].astype(F32).T
+
+    @pl.when(step == 0)
+    def _():
+        count = small_ref.shape[0]
+        pairs = [small_ref[2 * i] + small_ref[2 * i + 1] for i in range(count // 2)]
+        rows_ref[...] = sum(pairs[1:], pairs[0])
+        micros = conditions_ref.shape[0] // (count // 2)
+        for k in range(3):
+            rows = jnp.concatenate([pair[3 * m + k : 3 * m + k + 1] for pair in pairs for m in range(micros)], 0)
+            mod_weight_grad[:, k * features : (k + 1) * features] = lax.dot_general(
+                conditions_ref[...], rows, (((0,), (0,)), ((), ())), precision=HIGH, preferred_element_type=F32
+            )
+
+
+def place_gradients(first, second, small, conditions, hidden):
+    features = first.shape[2]
+    width = features // 2
+    cond = conditions.shape[1]
+    whole = lambda dims: pl.BlockSpec(dims, lambda i: (0,) * len(dims))
+    return pl.pallas_call(
+        place_kernel,
+        grid=(hidden // width,),
+        in_specs=[whole(first.shape), whole(second.shape), whole(small.shape), whole(conditions.shape)],
+        out_specs=[
+            pl.BlockSpec((features, width), lambda i: (0, i)),
+            pl.BlockSpec((width, features), lambda i: (i, 0)),
+            whole((cond, 3 * features)),
+            whole((SMALL_ROWS, features)),
+        ],
+        out_shape=(
+            shape((features, hidden), F32),
+            shape((hidden, features), F32),
+            shape((cond, 3 * features), F32),
+            shape((SMALL_ROWS, features), F32),
+        ),
+        compiler_params=params(),
+        name="place_gradients",
+    )(first, second, small, conditions)
 
 
 def rope_tables(length, core):
@@ -728,143 +1220,40 @@
         ),
         lambda: first.T,
     )
-    states, stream, kept_first, kept_second, kept_rows, back_first, back_second, sums = pipeline(
+    states, stream, kept_first, kept_second, kept_rows, back_first, back_second, sums, bias = pipeline(
         jnp.stack(enter_rows), jnp.stack(cot_rows), wide, second, mods_rows, gain, keep, bias_heads, in_bias,
         out_bias, cosine, sine,
     )
     states = states[None]
     stream = stream[None]
 
-    mid = hidden // 2
-
-    def attention_grads():
-        rows = kept_second[:, :, : 2 * features].reshape(micro_count, half, 2, features)
-        rows = rows.transpose(0, 2, 1, 3).reshape(micro_count * length, features)
-        mixed = kept_first[:, width:].reshape(micro_count, half - width, 3, length)
-        mixed = mixed.transpose(2, 1, 0, 3).reshape(width, micro_count * length)
-        grad_branch = back_second[:, :, : 2 * features].reshape(micro_count, half, 2, features)
-        grad_branch = grad_branch.transpose(0, 2, 1, 3).reshape(micro_count * length, features)
-        grad_proj = back_first[:, :width].reshape(micro_count, width, 3, length)
-        grad_proj = grad_proj.transpose(2, 1, 0, 3).reshape(3 * width, micro_count * length)
-        own = jnp.concatenate([dot_nn(grad_proj, rows), dot_nn(mixed, grad_branch)], 0)
-        zeros = jnp.zeros((mid, features), F32)
-        bias_in = jnp.sum(grad_proj.astype(F32), 1).reshape(3, width)
-        bias_out = jnp.sum(grad_branch.astype(F32).reshape(micro_count, 2, half, features)[:, 0], (0, 1))
-        low = jnp.where(core == 0, bias_in, 0.0)
-        high = jnp.where(core == 0, 0.0, bias_in)
-        bias = jnp.concatenate([jnp.concatenate([low, high], 1).reshape(3 * features), bias_out])
-        low_zeros = jnp.zeros((mid, features), BF16)
-        return own, zeros, low_zeros, low_zeros, bias, jnp.zeros((features,), F32)
-
-    def transposed_dot(left, right):
-        return lax.dot_general(left, right, (((0,), (0,)), ((), ())), preferred_element_type=F32)
-
-    def feed_grads():
-        rows = kept_rows.reshape(micro_count * half, features)
-        active = kept_second.reshape(micro_count * half, hidden)
-        grad_branch = back_second[:, :, :features].reshape(micro_count * half, features)
-        grad_hidden = back_first.reshape(micro_count * half, hidden)
-        grad_first = transposed_dot(grad_hidden, rows)
-        grad_second = transposed_dot(active, grad_branch)
-        pick_half = lambda array, which: lax.dynamic_slice_in_dim(array, which * mid, mid, 0)
-        return (
-            pick_half(grad_first, core),
-            pick_half(grad_second, core),
-            pick_half(grad_first, 1 - core).astype(BF16),
-            pick_half(grad_second, 1 - core).astype(BF16),
-            jnp.sum(grad_hidden.astype(F32), 0),
-            jnp.sum(grad_branch.astype(F32), 0),
-        )
-
-    own_first, own_second, send_first, send_second, bias_first, bias_second = lax.cond(
-        section % 2 == 0, attention_grads, feed_grads
-    )
-    odd = [s for s in every if s % 2 == 1]
-    own_first = own_first + swap_cores(send_first, odd).astype(F32)
-    own_second = own_second + swap_cores(send_second, odd).astype(F32)
-
-    bits = dp_count.bit_length() - 1
-    chip_bits = list(range(1, bits))
-
-    def swap_bit(value, bit, active):
-        return lax.ppermute(
-            value, AXES, [(flat(d, s), flat(d ^ (1 << bit), s)) for d in range(dp_count) for s in active]
-        )
-
-    def sum_over_chips(total, active):
-        columns = total.shape[1] // 2
-        results = []
-        for part, order in enumerate((chip_bits, chip_bits[::-1])):
-            piece = total[:, part * columns : (part + 1) * columns]
-            for bit in order:
-                size = piece.shape[0] // 2
-                low = ((dp_index >> bit) & 1) == 0
-                keep = jnp.where(low, piece[:size], piece[size:])
-                send = jnp.where(low, piece[size:], piece[:size]).astype(BF16)
-                piece = keep + swap_bit(send, bit, active).astype(F32)
-            piece = piece.astype(BF16)
-            for bit in order[::-1]:
-                low = ((dp_index >> bit) & 1) == 0
-                got = swap_bit(piece, bit, active)
-                piece = jnp.where(
-                    low, jnp.concatenate([piece, got], 0), jnp.concatenate([got, piece], 0)
-                )
-            results.append(piece)
-        return jnp.concatenate(results, 1)
-
-    sum_first = sum_over_chips(own_first, every)
-    sum_second = sum_over_chips(own_second, odd)
-    got_first = swap_cores(sum_first, every)
-    got_second = swap_cores(sum_second, odd)
-    low_first = jnp.where(core == 0, sum_first, got_first)
-    high_first = jnp.where(core == 0, got_first, sum_first)
-    low_second = jnp.where(core == 0, sum_second, got_second)
-    high_second = jnp.where(core == 0, got_second, sum_second)
-
-    def attention_whole():
-        columns = []
-        for block in range(3):
-            for side in (low_first, high_first):
-                columns.append(side[block * width : (block + 1) * width].T)
-        out_rows = jnp.concatenate([low_first[3 * width :], high_first[3 * width :]], 0)
-        return jnp.concatenate(columns + [out_rows], 1).astype(F32), jnp.zeros((hidden, features), F32)
-
-    def feed_whole():
-        return (
-            jnp.concatenate([low_first, high_first], 0).T.astype(F32),
-            jnp.concatenate([low_second, high_second], 0).astype(F32),
-        )
-
-    grad_in, grad_out = lax.cond(section % 2 == 0, attention_whole, feed_whole)
-
-    small = jnp.concatenate(
-        [sums[:, :3].reshape(-1), jnp.sum(sums[:, 3], 0), jnp.sum(sums[:, 4], 0), bias_first, bias_second]
-    )
-    packed = jnp.concatenate([small, time_step.astype(F32)])
-    gathered = lax.all_gather(packed, "dp")
-    pairs = gathered[:, : small.shape[0]].reshape(dp_count // 2, 2, -1).sum(1)
-    count = micro_count * 3 * features
-    grad_modulation = pairs[:, :count].reshape(dp_count // 2 * micro_count, 3 * features)
-    rest = jnp.sum(pairs[:, count:], 0)
-    steps_all = gathered[:, small.shape[0] :].astype(jnp.int32)
-    steps_all = steps_all.reshape(dp_count // 2, 2, seqs).transpose(0, 2, 1).reshape(-1)
+    steps_all = lax.all_gather(time_step, "dp").reshape(dp_count // 2, 2, seqs).transpose(0, 2, 1).reshape(-1)
     onehot_all = (
         steps_all[:, None] == lax.broadcasted_iota(jnp.int32, (steps_all.shape[0], time_table.shape[0]), 1)
     ).astype(F32)
     embedded_all = jnp.dot(onehot_all, time_table, precision=HIGH)
     conditions_all, silu_pull = jax.vjp(jax.nn.silu, embedded_all)
-    grad_mod_weight = jnp.dot(conditions_all.T, grad_modulation, precision=HIGH)
-    grad_mod_bias = jnp.sum(grad_modulation, 0)
-    grad_condition = lax.dot_general(
-        grad_modulation, mod_weight[0], (((1,), (1,)), ((), ())), precision=HIGH, preferred_element_type=F32
+
+    summed_first, summed_second, small = summed_gradients(
+        kept_first, kept_second, kept_rows, back_first, back_second, sums, bias, mod_weight[0], dp_count
     )
-    grad_gain = rest[:features]
-    embed_total = jnp.where(is_first, rest[features : 2 * features], 0.0)
-    grad_bias_first = rest[2 * features : 2 * features + hidden]
-    grad_bias_second = rest[2 * features + hidden :]
-    across = lax.psum(jnp.concatenate([grad_condition.reshape(-1), embed_total]), "section")
-    grad_condition = across[: grad_condition.size].reshape(grad_condition.shape)
-    embed_total = across[grad_condition.size :]
+    base = 3 * micro_count
+    blocks = hidden // features
+    cross = small[:, base + blocks + 2 : base + blocks + 4].reshape(dp_count // 2, 2, 2, features).sum(1)
+    turns = [
+        lax.ppermute(cross, "section", [(s, (s + turn) % sections) for s in every]) for turn in range(1, sections)
+    ]
+    grad_in, grad_out, grad_mod_weight, rows = place_gradients(
+        summed_first, summed_second, small, conditions_all, hidden
+    )
+    grad_mod_bias = jnp.sum(rows[: 3 * micro_count].reshape(micro_count, 3 * features), 0)
+    grad_gain = rows[base]
+    grad_bias_first = rows[base + 1 : base + 1 + blocks].reshape(hidden)
+    grad_bias_second = rows[base + 1 + blocks]
+    cross = sum(turns, cross)
+    cond = time_table.shape[1]
+    grad_condition = cross[:, 0, : micro_count * cond].reshape(-1, cond)
+    embed_total = jnp.sum(cross[:, 1], 0)
     grad_embedded = silu_pull(grad_condition)[0]
     table_total = lax.dot_general(
         onehot_all, grad_embedded, (((0,), (0,)), ((), ())), precision=HIGH, preferred_element_type=F32

time: 791 us -> 488 us (0.62)
  local copies, waits for them, and re-layouts: 232 us -> 29.3 us
  Pallas kernels: 304 us -> 401 us
  waiting for transfers between devices: 80.5 us -> 0.02 us
  other arithmetic: 63.2 us -> 24.6 us
  matrix products: 27.9 us -> 4.16 us
  starting transfers between devices: 30 us -> 10.8 us
  between operations: 15.6 us -> 2.13 us
  blocking collectives: 20.2 us -> 9.46 us
    pallas_call x0 -> x2, Pallas kernels: none -> 97 us  [the longest x1 84.1 us: summed_gradients(): pl.pallas_call(gradient_kernel, in_specs=[anywhere] * 5 + [inside] * 3, o...]
    another operation x11 -> x1, local copies, waits for them, and re-layouts: 77.9 us -> 0.01 us
    unnamed x2 -> x0, waiting for transfers between devices: 50.6 us -> none
    transpose x5 -> x1, local copies, waits for them, and re-layouts: 39.7 us -> 0.11 us  [shards(): lax.all_gather(time_step, 'dp').reshape(dp_count // 2, 2, seqs)]
    cond x9 -> x2, local copies, waits for them, and re-layouts: 32.3 us -> 0.29 us
    ppermute x16 -> x3, waiting for transfers between devices: 29.9 us -> 0.01 us  [shards(): lax.ppermute(cross, 'section', [(s, (s + turn) % sections) for s in every])]
    slice x11 -> x3, local copies, waits for them, and re-layouts: 31 us -> 2.15 us  [the longest x1 1.34 us: shards(): grad_bias_second = rows[base + 1 + blocks]]
    dot_general x4 -> x0, matrix products: 24 us -> none  [the longest x2 19 us: dot_nn(): return jnp.dot(left, right, preferred_element_type=F32)]
  transfers between devices with their start and end apart: 26 -> 8, of which waited for: 7 -> 0; matrix products, arithmetic and copies ran while one was open for 11% -> 8% of each run, Pallas kernels for 0% -> 3%
where the time goes in v2:
time: 488 us; the launch traced here: 481 us
  Pallas kernels  401 us (82%)
  local copies, waits for them, and re-layouts  29.3 us (6%)
  other arithmetic  24.6 us (5%)
  starting transfers between devices  10.8 us (2%)
  blocking collectives  9.46 us (2%)
    pallas_call x1, Pallas kernels, pipeline(): pl.pallas_call(pipeline_kernel, in_specs=[anywhere] * 4 + [inside] * 8, o...  304 us
    pallas_call x1, Pallas kernels, summed_gradients(): pl.pallas_call(gradient_kernel, in_specs=[anywhere] * 5 + [inside] * 3, o...  84.1 us
    pallas_call x1, Pallas kernels, place_gradients(): pl.pallas_call(place_kernel, grid=(hidden // width,), in_specs=[whole(fir...  12.9 us
  transfers between devices with their start and end apart: 8, of which 0 were waited for; matrix products, arithmetic and copies ran while one was open for 8% of the time, Pallas kernels for 3%

profile of v2, /device:TPU:0, one launch (start us, length us, event | category | flops | bytes accessed | tf_op | source)
XLA Modules:
  0.0 481.1 jit_solution(2049275925843326329)
XLA Ops:
  2.1 2.1 broadcast_select_fusion
  5.6 2.5 collective-permute-start
  8.1 2.0 collective-permute-start.1
  11.3 1.8 collective-permute-start.2
  13.1 2.3 collective-permute-start.4
  15.8 1.9 convolution_add_fusion
  17.9 2.7 constant_dynamic-slice_fusion.9
  20.6 2.1 copy.39
  22.7 2.1 copy.40
  26.3 2.1 copy.41
  28.4 9.5 %all-reduce.1 = s32[16]{0:T(128)S(1)} all-reduce(s32[16]{0:T(128)S(1)} %dynamic-update-slice), channel_id=2, replica_groups=mesh['dp'=8,'section'=4] {'dp'}, use_global_device_ids=true, to_apply=%add.1 | all-reduce | flops 16 | bytes 128
  39.0 2.7 maximum_bitcast_fusion
  43.9 9.0 %conditional.1 = (bf16[3072,768]{1,0:T(8,128)(2,1)}) conditional(s32[]{:T(128)} %convert_element_type.11, (bf16[768,3072]{1,0:T(8,128)(2,1)}) %tuple.56, (bf16[768,3072]{1,0:T(8,128)(2,1)}, pred[]{:T(512)}, s32[]{:T(128)}, s32[]{:T(128)}, s32[]{:T(128)}, /*index=5*/bf16[1152,768]{1,0:T(8,128)(2,1)}) %tuple.57), branch_computations={%region_0.1_spmd, %region_1.2_spmd} | conditional | flops 18874372 | bytes 19481196 | solution.py:1216
  43.9 2.4 slice.15
  48.1 4.7 maximum_maximum_fusion
  54.3 2.3 broadcast_select_fusion.5.keep_ref
  57.2 2.1 select_bitcast_fusion.3
  59.6 2.0 broadcast_select_fusion.4
  61.6 3.6 pad_maximum_fusion
  66.2 303.5 %pipeline.1 = (bf16[2,1024,768]{2,1,0:T(8,128)(2,1)}, bf16[2,1024,768]{2,1,0:T(8,128)(2,1)}, bf16[4,512,3072]{2,1,0:T(8,128)(2,1)}, bf16[4,512,3072]{2,1,0:T(8,1...) custom-call(bf16[4,512,768]{2,1,0:T(8,128)(2,1)} %get-tuple-element., ...), custom_call_target="tpu_custom_call" | custom-call | tf_op jit(solution)/shard_map/pipeline/pallas_call | solution.py:600
  369.7 84.1 %summed_gradients.1 = (bf16[2,1536,768]{2,1,0:T(8,128)(2,1)}, bf16[2,1536,768]{2,1,0:T(8,128)(2,1)}, f32[8,24,768]{2,1,0:T(8,128)}) custom-call(bf16[4,512,3072]{2,1,0:T(8,128)(2,1)} %get-tuple-element.109.kept_first, bf16[4,512,3072]{2,1,0:T(8,128)(2,1)} %get-tuple-element.110.kept_second, bf16[4,512,768]{2,1,0:T(8,128)(2,1)} %get-tuple-element.111.kept_rows, ...), custom_call_target="tpu_custom_call" | custom-call | tf_op jit(solution)/shard_map/summed_gradients/pallas_call | solution.py:1018
  455.0 2.0 collective-permute-start.5
  456.9 12.9 %place_gradients.1 = (f32[768,3072]{1,0:T(8,128)}, f32[3072,768]{1,0:T(8,128)}, f32[128,2304]{1,0:T(8,128)}, f32[24,768]{1,0:T(8,128)}) custom-call(bf16[2,1536,768]{2,1,0:T(8,128)(2,1)} %get-tuple-element.117.first_ref, bf16[2,1536,768]{2,1,0:T(8,128)(2,1)} %get-tuple-element.118.second_ref, f32[8,24,768]{2,1,0:T(8,128)} %get-tuple-element.116.small_ref, ...), custom_call_target="tpu_custom_call" | custom-call | tf_op jit(solution)/shard_map/place_gradients/pallas_call | solution.py:1102
  475.9 1.7 copy.57
  (82 shorter events, 23.8 us)
Async XLA Ops:
  0.6 14.9 %copy-start = (f32[512,128]{1,0:T(8,128)S(1)}, f32[512,128]{1,0:T(8,128)}, u32[]{:S(2)}) copy-start(f32[512,128]{1,0:T(8,128)} %param.20) | copy-start | bytes 786436
  4.3 5.8 %copy-start.5 = (bf16[2,1024,768]{2,1,0:T(8,128)(2,1)S(1)}, bf16[2,1024,768]{2,1,0:T(8,128)(2,1)}, u32[]{:S(2)}) copy-start(bf16[2,1024,768]{2,1,0:T(8,128)(2,1)} %param.29) | copy-start | bytes 9437188
  4.3 11.2 %copy-start.7 = (f32[1,2304]{1,0:T(1,128)S(1)}, f32[1,2304]{1,0:T(1,128)}, u32[]{:S(2)}) copy-start(f32[1,2304]{1,0:T(1,128)} %param.23) | copy-start | bytes 27652
  4.3 11.2 %copy-start.8 = (s32[2]{0:T(128)S(1)}, s32[2]{0:T(128)}, u32[]{:S(2)}) copy-start(s32[2]{0:T(128)} %param.19) | copy-start | bytes 28
  5.6 51.6 %collective-permute-start = (bf16[512,768]{1,0:T(8,128)(2,1)}, bf16[512,768]{1,0:T(8,128)(2,1)}, u32[]{:S(2)}, u32[]{:S(2)}) collective-permute-start(bf16[512,768]{1,0:T(8,128)(2,1)} %get-tuple-element.144), channel_id=1, source_target_pairs={{0,4},{4,0},{8,12},{12,8},{16,20},{20,16},{24,28},{28,24}} | collective-permute-start | bytes 2359304 | tf_op jit(solution)/shard_map/ppermute | solution.py:1155
  8.1 49.2 %collective-permute-start.1 = (bf16[512,768]{1,0:T(8,128)(2,1)}, bf16[512,768]{1,0:T(8,128)(2,1)}, u32[]{:S(2)}, u32[]{:S(2)}) collective-permute-start(bf16[512,768]{1,0:T(8,128)(2,1)} %get-tuple-element.145), channel_id=1, source_target_pairs={{0,4},{4,0},{8,12},{12,8},{16,20},{20,16},{24,28},{28,24}} | collective-permute-start | bytes 2359304 | tf_op jit(solution)/shard_map/ppermute | solution.py:1155
  11.3 48.0 %collective-permute-start.2 = (bf16[2,512,768]{2,1,0:T(8,128)(2,1)}, bf16[2,512,768]{2,1,0:T(8,128)(2,1)}, u32[]{:S(2)}, u32[]{:S(2)}) collective-permute-start(bf16[2,512,768]{2,1,0:T(8,128)(2,1)} %constant_dynamic-slice_fusion.10), channel_id=1, source_target_pairs={{3,7},{7,3},{11,15},{15,11},{19,23},{23,19},{27,31},{31,27}} | collective-permute-start | bytes 4718600 | tf_op jit(solution)/shard_map/ppermute | solution.py:1155
  13.1 39.7 %collective-permute-start.4 = (f32[2,512]{1,0:T(2,128)S(1)}, f32[2,512]{1,0:T(2,128)S(1)}, u32[]{:S(2)}, u32[]{:S(2)}) collective-permute-start(f32[2,512]{1,0:T(2,128)S(1)} %constant_dynamic-slice_fusion.6), channel_id=1, source_target_pairs={{0,4},{4,0},{8,12},{12,8},{16,20},{20,16},{24,28},{28,24}} | collective-permute-start | bytes 12296 | tf_op jit(solution)/shard_map/ppermute | solution.py:1155
  17.7 7.1 %copy-start.9 = (u32[32]{0:T(128)S(1)}, u32[32]{0:T(128)}, u32[]{:S(2)}) copy-start(u32[32]{0:T(128)} %constant.92) | copy-start | bytes 388
  17.7 38.8 %collective-permute-start.3 = (f32[2,3,768]{2,1,0:T(4,128)S(1)}, f32[2,3,768]{2,1,0:T(4,128)S(1)}, u32[]{:S(2)}, u32[]{:S(2)}) collective-permute-start(f32[2,3,768]{2,1,0:T(4,128)S(1)} %reshape.150), channel_id=1, source_target_pairs={{0,4},{1,5},{2,6},{3,7},{4,0},{5,1},{6,2},{7,3},{8,12},{9,13},{10,... | collective-permute-start | bytes 55304 | tf_op jit(solution)/shard_map/ppermute | solution.py:1155
  46.3 1.8 copy-start.2
  57.2 2.4 copy-start.6
  61.5 4.6 slice-start
  61.6 4.6 slice-start.1
  454.8 19.2 %collective-permute-start.7 = (f32[4,2,768]{2,1,0:T(2,128)S(1)}, f32[4,2,768]{2,1,0:T(2,128)S(1)}, u32[]{:S(2)}, u32[]{:S(2)}) collective-permute-start(f32[4,2,768]{2,1,0:T(2,128)S(1)} %bitcast_reduce_fusion), channel_id=1, source_target_pairs={{0,3},{1,0},{2,1},{3,2},{4,7},{5,4},{6,5},{7,6},{8,11},{9,8},{10,9... | collective-permute-start | bytes 73736 | tf_op jit(solution)/shard_map/ppermute | solution.py:1244
  454.9 19.2 %collective-permute-start.6 = (f32[4,2,768]{2,1,0:T(2,128)S(1)}, f32[4,2,768]{2,1,0:T(2,128)S(1)}, u32[]{:S(2)}, u32[]{:S(2)}) collective-permute-start(f32[4,2,768]{2,1,0:T(2,128)S(1)} %bitcast_reduce_fusion), channel_id=1, source_target_pairs={{0,2},{1,3},{2,0},{3,1},{4,6},{5,7},{6,4},{7,5},{8,10},{9,11},{10,... | collective-permute-start | bytes 73736 | tf_op jit(solution)/shard_map/ppermute | solution.py:1244
  455.0 19.1 %collective-permute-start.5 = (f32[4,2,768]{2,1,0:T(2,128)S(1)}, f32[4,2,768]{2,1,0:T(2,128)S(1)}, u32[]{:S(2)}, u32[]{:S(2)}) collective-permute-start(f32[4,2,768]{2,1,0:T(2,128)S(1)} %bitcast_reduce_fusion), channel_id=1, source_target_pairs={{0,1},{1,2},{2,3},{3,0},{4,5},{5,6},{6,7},{7,4},{8,9},{9,10},{10,1... | collective-permute-start | bytes 73736 | tf_op jit(solution)/shard_map/ppermute | solution.py:1244
  456.9 18.9 %copy-start.4 = (bf16[2,1024,768]{2,1,0:T(8,128)(2,1)S(1)}, bf16[2,1024,768]{2,1,0:T(8,128)(2,1)}, u32[]{:S(2)}) copy-start(bf16[2,1024,768]{2,1,0:T(8,128)(2,1)} %get-tuple-element.107) | copy-start | bytes 9437188
  475.9 3.0 copy-start.3
  475.9 4.7 copy-start.1
